TPU v7x, 128 devices: a whole 4x4x4 slice. The times are simulated.
128 devices in a mesh: wide: 16 (over z, x), narrow: 8 (over y, core).
Axes of the slice: x: 4, y: 4, z: 4, core: 2. Of those that a mesh axis runs over, the one named last changes fastest.
Arguments:
- tokens: bfloat16 [1024, 12288], P('narrow'), may hold values from -6 to 6
- first_blocks: bfloat16 [384, 40, 128, 128], P('wide', 'narrow'), may hold values from -0.109375 to 0.109375
- second_blocks: bfloat16 [384, 40, 128, 128], P('wide', 'narrow'), may hold values from -0.0546875 to 0.0546875
- block_rows: int32 [384, 40], P('wide', 'narrow'), may hold values from 0 to 11, as said below
- block_count: int32 [384, 8], P('wide', 'narrow'), may hold values from 1 to 5, as said below
- upstream: bfloat16 [1024, 12288], P('narrow'), may hold values from -1.5 to 1.5
Outputs:
- layer_output: bfloat16 [1024, 12288], P('wide', 'narrow')
- grad_tokens: bfloat16 [1024, 12288], P('wide', 'narrow')
- first_grad: float32 [384, 40, 128, 128], P('wide', 'narrow')
- second_grad: float32 [384, 40, 128, 128], P('wide', 'narrow')
Inputs may be any that keep to these rules, and one draw needn't show every extreme that they name: `block_rows`: within each panel and each group of 5 slots the values are distinct. The first block_count slots of a panel's group are kept; in every group some panel keeps all 5.
All inputs are finite; a program needn't handle non-finite values.
Results may differ from a plain program's by a relative error of at most 0.029.
Values may be sent and summed in bfloat16 or wider, within the bound.
A program may use at most 320 MiB of HBM per device.

v0:
```python
import math

import jax
import jax.numpy as jnp
from jax import lax
from jax.sharding import PartitionSpec as P


def on_device(tokens, first_blocks, second_blocks, block_rows, block_count, upstream):
    wide_size = lax.axis_size("wide")
    narrow_size = lax.axis_size("narrow")
    panels, capacity, block_size, _ = first_blocks.shape
    width_total = tokens.shape[1]
    group_blocks = width_total // narrow_size // block_size
    kept_mask = jnp.arange(capacity, dtype=jnp.int32)[None, :] < block_count
    kept_blocks = kept_mask[:, :, None, None]
    first_kept = jnp.where(kept_blocks, first_blocks, jnp.zeros((), jnp.bfloat16))
    second_kept = jnp.where(kept_blocks, second_blocks, jnp.zeros((), jnp.bfloat16))
    block_selector = (
        block_rows[:, :, None] == jnp.arange(group_blocks, dtype=jnp.int32)[None, None, :]
    ).astype(jnp.bfloat16)
    token_all, upstream_all = (
        lax.all_to_all(tokens, "narrow", split_axis=1, concat_axis=0, tiled=True),
        lax.all_to_all(upstream, "narrow", split_axis=1, concat_axis=0, tiled=True),
    )
    token_count = token_all.shape[0]
    token_slots = jnp.take(
        token_all.reshape(token_count, group_blocks, block_size), block_rows, axis=1
    )
    upstream_slots = jnp.take(
        upstream_all.reshape(token_count, group_blocks, block_size), block_rows, axis=1
    )

    def hidden_sum(slots, weight_matrices, pattern):
        product = jnp.einsum(pattern, slots, weight_matrices, preferred_element_type=jnp.float32)
        return lax.psum_scatter(
            product.reshape(
                lax.axis_size("narrow") * (token_count // narrow_size), panels * block_size
            ).astype(jnp.bfloat16),
            "narrow",
            scatter_dimension=0,
            tiled=True,
        ).astype(jnp.float32)

    def hidden_rows(share):
        return lax.all_gather(share, "narrow", axis=0, tiled=True)

    def width_sum(source, weight_matrices, pattern):
        amount = lax.axis_size("wide") * (token_count // wide_size)
        row_segment = source.reshape(amount, panels, block_size)
        step_rows = math.gcd(amount, 512)

        def apply_block(rows_block):
            product = jnp.einsum(
                pattern, rows_block, weight_matrices, preferred_element_type=jnp.float32
            )
            upper_bound = product.astype(jnp.bfloat16)
            lower_bound = (product - upper_bound.astype(jnp.float32)).astype(jnp.bfloat16)
            placed = jnp.einsum(
                "svob,voy->syb", upper_bound, block_selector, preferred_element_type=jnp.float32
            )
            placed = placed + jnp.einsum(
                "svob,voy->syb", lower_bound, block_selector, preferred_element_type=jnp.float32
            )
            return placed.reshape(step_rows, group_blocks * block_size)

        results = lax.map(
            apply_block, row_segment.reshape(amount // step_rows, step_rows, panels, block_size)
        )
        return lax.psum_scatter(
            results.reshape(amount, group_blocks * block_size).astype(jnp.bfloat16),
            "wide",
            scatter_dimension=0,
            tiled=True,
        ).astype(jnp.float32)

    preact = hidden_sum(token_slots, first_kept, "tpck,pckf->tpf")
    hidden_portion = jax.nn.gelu(preact).astype(jnp.bfloat16)
    hidden_all = hidden_rows(hidden_portion)
    layer_output = width_sum(hidden_all, second_kept, "tpf,pcfk->tpck").astype(jnp.bfloat16)
    hidden_gradient = hidden_sum(upstream_slots, second_kept, "tpck,pcfk->tpf")
    pullback = jax.vjp(jax.nn.gelu, preact)[1]
    grad_pre = pullback(hidden_gradient)[0].astype(jnp.bfloat16)
    grad_all = hidden_rows(grad_pre)
    hidden_panels = hidden_all.reshape(token_count, panels, block_size)
    grad_panels = grad_all.reshape(token_count, panels, block_size)
    second_grad = jnp.where(
        kept_blocks,
        jnp.einsum(
            "tpf,tpck->pcfk", hidden_panels, upstream_slots, preferred_element_type=jnp.float32
        ),
        0.0,
    )
    first_grad = jnp.where(
        kept_blocks,
        jnp.einsum("tpck,tpf->pckf", token_slots, grad_panels, preferred_element_type=jnp.float32),
        0.0,
    )
    grad_tokens = width_sum(grad_all, first_kept, "tpf,pckf->tpck").astype(jnp.bfloat16)
    return (layer_output, grad_tokens, first_grad, second_grad)


def solution(mesh):
    in_specs = (
        P("narrow", None),
        P("wide", "narrow", None, None),
        P("wide", "narrow", None, None),
        P("wide", "narrow"),
        P("wide", "narrow"),
        P("narrow", None),
    )
    out_specs = (
        P("wide", "narrow"),
        P("wide", "narrow"),
        P("wide", "narrow", None, None),
        P("wide", "narrow", None, None),
    )
    return jax.shard_map(
        on_device, mesh=mesh, in_specs=in_specs, out_specs=out_specs, check_vma=False
    )
```

profile of v0, /device:TPU:2, one launch (start us, length us, event | category | flops | bytes accessed | tf_op | source)
XLA Modules:
  0.0 767.1 jit_solution(12117050786698228819)
XLA Ops:
  7.2 4.6 copy.57
  11.8 4.6 all-to-all-start
  17.5 5.5 broadcast_select_fusion.7
  23.0 31.9 %all-to-all-done = bf16[128,8,1536]{0,2,1:T(8,128)(2,1)S(1)} async-done(((bf16[128,8,1536]{0,2,1:T(8,128)(2,1)}), bf16[128,8,1536]{0,2,1:T(8,128)(2,1)S(1)}, u32[]{:S(2)}, u32[]{:S(2)}) %all-to-all-start) | async-done | bytes 3145760 | tf_op jit(solution)/shard_map/all_to_all | solution.py:23
  54.8 10.1 %copy.58 = bf16[8,128,1536]{1,0,2:T(8,128)(2,1)} copy(bf16[8,128,1536]{1,2,0:T(8,128)(2,1)S(1)} %bitcast.166) | data formatting | bytes 6291456 | tf_op jit(solution)/shard_map/all_to_all | solution.py:23
  64.9 5.8 reshape.68
  70.7 3.5 copy.60
  74.2 12.3 %gather_fusion = bf16[120,1024,128]{2,1,0:T(8,128)(2,1)} fusion(bf16[1024,12,128]{2,0,1:T(8,128)(2,1)S(1)} %copy.60, s32[1024]{0:T(1024)S(1)} %pad_clamp_fusion), kind=kCustom, calls=%fused_computation.clone | custom fusion | bytes 62915040 | tf_op jit(solution)/shard_map/jit(_take)/gather | solution.py:27
  86.4 40.8 %copy.61 = bf16[24,5,1024,128]{2,3,1,0:T(8,128)(2,1)} copy(bf16[24,5,1024,128]{3,2,1,0:T(8,128)(2,1)} %bitcast.162) | data formatting | bytes 62914560 | tf_op jit(solution)/shard_map/jit(_take)/gather | solution.py:27
  127.2 16.1 %bitcast_convert_fusion.3 = bf16[24,128,1024]{2,1,0:T(8,128)(2,1)} fusion(bf16[24,5,128,128]{3,2,1,0:T(8,128)(2,1)} %get-tuple-element.238, bf16[24,5,1024,128]{2,3,1,0:T(8,128)(2,1)} %copy.61, pred[24,5]{1,0:T(8,128)(4,1)S(1)} %copy.56), kind=kOutput, calls=%fused_computation.57 | convolution fusion | flops 4045406208 | bytes 41681016 | tf_op jit(solution)/shard_map/tpck,pckf->tpf/dot_general | solution.py:35
  143.3 8.7 %copy.101 = bf16[1024,3072]{1,0:T(8,128)(2,1)} copy(bf16[1024,3072]{0,1:T(8,128)(2,1)} %bitcast.173) | data formatting | bytes 12582912
  152.0 3.5 copy.68
  155.5 57.4 %all_to_all.32 = bf16[128,8,1536]{0,2,1:T(8,128)(2,1)S(1)} all-to-all(bf16[128,8,1536]{0,2,1:T(8,128)(2,1)S(1)} %bitcast.170), channel_id=1, replica_groups=mesh['wide'=16,'narrow'=8] {'narrow'}, dimensions={1} | all-to-all | bytes 6291456 | tf_op jit(solution)/shard_map/all_to_all | solution.py:24
  212.9 8.9 %copy.69 = bf16[8,128,1536]{1,0,2:T(8,128)(2,1)S(1)} copy(bf16[8,128,1536]{1,2,0:T(8,128)(2,1)S(1)} %bitcast.169) | data formatting | bytes 6291456 | tf_op jit(solution)/shard_map/all_to_all | solution.py:24
  221.8 3.3 reshape.69
  225.2 3.5 copy.71
  228.7 12.3 %gather_fusion.1 = bf16[120,1024,128]{2,1,0:T(8,128)(2,1)} fusion(bf16[1024,12,128]{2,0,1:T(8,128)(2,1)S(1)} %copy.71, s32[1024]{0:T(1024)S(1)} %pad_clamp_fusion), kind=kCustom, calls=%fused_computation.1.clone | custom fusion | bytes 62915040 | tf_op jit(solution)/shard_map/jit(_take)/gather | solution.py:30
  240.9 40.7 %copy.72 = bf16[24,5,1024,128]{2,3,1,0:T(8,128)(2,1)} copy(bf16[24,5,1024,128]{3,2,1,0:T(8,128)(2,1)} %bitcast.161) | data formatting | bytes 62914560 | tf_op jit(solution)/shard_map/jit(_take)/gather | solution.py:30
  281.6 16.4 %bitcast_convert_fusion.2 = bf16[24,128,1024]{2,1,0:T(8,128)(2,1)} fusion(bf16[24,5,128,128]{3,2,1,0:T(8,128)(2,1)} %get-tuple-element.220, bf16[24,5,1024,128]{2,3,1,0:T(8,128)(2,1)} %copy.72, pred[24,5]{1,0:T(8,128)(4,1)S(1)} %copy.56), kind=kOutput, calls=%fused_computation.56 | convolution fusion | flops 4045406208 | bytes 41681016 | tf_op jit(solution)/shard_map/tpck,pcfk->tpf/dot_general | solution.py:35
  298.0 8.6 %copy.103 = bf16[1024,3072]{1,0:T(8,128)(2,1)} copy(bf16[1024,3072]{0,1:T(8,128)(2,1)} %bitcast.174) | data formatting | bytes 12582912
  308.3 41.6 %reduce-scatter.15.cloned.1.call-done = bf16[128,3072]{1,0:T(8,128)(2,1)} async-done(((bf16[1024,3072]{1,0:T(8,128)(2,1)}), bf16[128,3072]{1,0:T(8,128)(2,1)}) %reduce-scatter.15.cloned.1.call-update) | async-done | bytes 786448
  354.5 44.2 %all-gather.5.cloned.1.call-done = bf16[1024,3072]{0,1:T(8,128)(2,1)} async-done(((bf16[128,3072]{0,1:T(8,128)(2,1)}), bf16[1024,3072]{0,1:T(8,128)(2,1)}) %all-gather.5.cloned.1.call-update) | async-done | bytes 6291472 | tf_op jit(solution)/shard_map/all_gather | solution.py:46
  398.7 11.1 %reshape.113 = bf16[2,512,24,128]{1,0,3,2:T(2,128)(2,1)} reshape(bf16[1024,3072]{0,1:T(8,128)(2,1)} %all-gather.5.cloned.1.call-done) | data formatting | bytes 12582912 | tf_op jit(solution)/shard_map/reshape;reshape | solution.py:68
  409.8 16.3 %copy.75 = bf16[2,512,24,128]{3,1,2,0:T(8,128)(2,1)} copy(bf16[2,512,24,128]{1,0,3,2:T(2,128)(2,1)} %reshape.113) | data formatting | bytes 12582912
  428.0 101.8 %while.23 = (s32[]{:T(128)}, bf16[2,512,1536]{1,2,0:T(8,128)(2,1)}, bf16[2,512,24,128]{3,1,2,0:T(8,128)(2,1)}, bf16[24,5,128,128]{3,2,1,0:T(8,128)(2,1)}, s32[24,5]{0,1:T(8,128)S(1)}, /*index=5*/s32[]{:T(128)}) while((s32[]{:T(128)}, bf16[2,512,1536]{1,2,0:T(8,128)(2,1)}, bf16[2,512,24,128]{3,1,2,0:T(8,128)(2,1)}, ...), condition=%wide.region_6.8_spmd.clone, body=%wide.region_5.7_spmd.clone.sunk | while | flops 2423789056 | bytes 84150280 | solution.py:67
  428.3 14.9 %fusion.110 = (bf16[512,24,5,128]{3,0,2,1:T(8,128)(2,1)}, bf16[512,24,5,128]{3,0,2,1:T(8,128)(2,1)}) fusion(bf16[24,5,128,128]{3,2,1,0:T(8,128)(2,1)} %get-tuple-element.250, bf16[2,512,24,128]{3,1,2,0:T(8,128)(2,1)} %get-tuple-element.249, s32[]{:T(128)} %get-tuple-element.241), kind=kOutput, calls=%fused_computation.25.clone.1 | convolution fusion | flops 2044723200 | bytes 38535680 | tf_op jit(solution)/shard_map/while/body/eval_jaxpr/tpf,pckf->tpck/dot_general | solution.py:54
  443.2 15.9 %fusion.111 = f32[512,128,12,1]{1,2,3,0:T(8,128)S(1)} fusion(bf16[512,24,5,128]{3,0,2,1:T(8,128)(2,1)} %get-tuple-element.215, s32[24,5]{0,1:T(8,128)S(1)} %get-tuple-element.251), kind=kOutput, calls=%fused_computation.26.clone.1 | convolution fusion | flops 188746560 | bytes 18874848 | tf_op jit(solution)/shard_map/while/body/eval_jaxpr/svob,voy->syb/dot_general | solution.py:62
  459.1 15.6 %fusion.112 = bf16[512,12,128]{2,1,0:T(8,128)(2,1)} fusion(f32[512,128,12,1]{1,2,3,0:T(8,128)S(1)} %fusion.111, bf16[512,24,5,128]{3,0,2,1:T(8,128)(2,1)} %get-tuple-element.216, s32[24,5]{0,1:T(8,128)S(1)} %get-tuple-element.251), kind=kOutput, calls=%fused_computation.31.clone.1 | convolution fusion | flops 190319424 | bytes 20447712 | tf_op jit(solution)/shard_map/while/body/eval_jaxpr/svob,voy->syb/dot_general | solution.py:59
  479.3 14.8 %fusion.110 = (bf16[512,24,5,128]{3,0,2,1:T(8,128)(2,1)}, bf16[512,24,5,128]{3,0,2,1:T(8,128)(2,1)}) fusion(bf16[24,5,128,128]{3,2,1,0:T(8,128)(2,1)} %get-tuple-element.250, bf16[2,512,24,128]{3,1,2,0:T(8,128)(2,1)} %get-tuple-element.249, s32[]{:T(128)} %get-tuple-element.241), kind=kOutput, calls=%fused_computation.25.clone.1 | convolution fusion | flops 2044723200 | bytes 38535680 | tf_op jit(solution)/shard_map/while/body/eval_jaxpr/tpf,pckf->tpck/dot_general | solution.py:54
  494.1 15.6 %fusion.111 = f32[512,128,12,1]{1,2,3,0:T(8,128)S(1)} fusion(bf16[512,24,5,128]{3,0,2,1:T(8,128)(2,1)} %get-tuple-element.215, s32[24,5]{0,1:T(8,128)S(1)} %get-tuple-element.251), kind=kOutput, calls=%fused_computation.26.clone.1 | convolution fusion | flops 188746560 | bytes 18874848 | tf_op jit(solution)/shard_map/while/body/eval_jaxpr/svob,voy->syb/dot_general | solution.py:62
  509.7 15.6 %fusion.112 = bf16[512,12,128]{2,1,0:T(8,128)(2,1)} fusion(f32[512,128,12,1]{1,2,3,0:T(8,128)S(1)} %fusion.111, bf16[512,24,5,128]{3,0,2,1:T(8,128)(2,1)} %get-tuple-element.216, s32[24,5]{0,1:T(8,128)S(1)} %get-tuple-element.251), kind=kOutput, calls=%fused_computation.31.clone.1 | convolution fusion | flops 190319424 | bytes 20447712 | tf_op jit(solution)/shard_map/while/body/eval_jaxpr/svob,voy->syb/dot_general | solution.py:59
  525.3 3.3 copy.128
  529.8 4.6 copy.76
  534.6 11.1 %reshape.112 = bf16[2,512,24,128]{1,0,3,2:T(2,128)(2,1)} reshape(bf16[1024,3072]{0,1:T(8,128)(2,1)} %all-gather.3.cloned.1.call-done) | data formatting | bytes 12582912 | tf_op jit(solution)/shard_map/reshape;reshape | solution.py:68
  545.7 16.2 %copy.65 = bf16[2,512,24,128]{3,1,2,0:T(8,128)(2,1)} copy(bf16[2,512,24,128]{1,0,3,2:T(2,128)(2,1)} %reshape.112) | data formatting | bytes 12582912
  563.8 114.9 %while.22 = (s32[]{:T(128)}, bf16[2,512,1536]{1,2,0:T(8,128)(2,1)}, bf16[2,512,24,128]{3,1,2,0:T(8,128)(2,1)}, bf16[24,5,128,128]{3,2,1,0:T(8,128)(2,1)}, s32[24,5]{0,1:T(8,128)S(1)}, /*index=5*/s32[]{:T(128)}) while((s32[]{:T(128)}, bf16[2,512,1536]{1,2,0:T(8,128)(2,1)}, bf16[2,512,24,128]{3,1,2,0:T(8,128)(2,1)}, ...), condition=%wide.region_2.4_spmd.clone, body=%wide.region_1.3_spmd.clone.sunk | while | flops 2423789056 | bytes 84150280 | solution.py:67
  576.3 15.4 %fusion.102 = (bf16[512,24,5,128]{3,0,2,1:T(8,128)(2,1)}, bf16[512,24,5,128]{3,0,2,1:T(8,128)(2,1)}) fusion(bf16[24,5,128,128]{3,2,1,0:T(8,128)(2,1)} %get-tuple-element.232, bf16[2,512,24,128]{3,1,2,0:T(8,128)(2,1)} %get-tuple-element.231, s32[]{:T(128)} %get-tuple-element.223), kind=kOutput, calls=%fused_computation.6.clone.1 | convolution fusion | flops 2044723200 | bytes 38535680 | tf_op jit(solution)/shard_map/while/body/eval_jaxpr/tpf,pcfk->tpck/dot_general | solution.py:54
  591.7 15.6 %fusion.103 = f32[512,128,12,1]{1,2,3,0:T(8,128)S(1)} fusion(bf16[512,24,5,128]{3,0,2,1:T(8,128)(2,1)} %get-tuple-element.208, s32[24,5]{0,1:T(8,128)S(1)} %get-tuple-element.233), kind=kOutput, calls=%fused_computation.7.clone.1 | convolution fusion | flops 188746560 | bytes 18874848 | tf_op jit(solution)/shard_map/while/body/eval_jaxpr/svob,voy->syb/dot_general | solution.py:62
  607.3 15.7 %fusion.104 = bf16[512,12,128]{2,1,0:T(8,128)(2,1)} fusion(f32[512,128,12,1]{1,2,3,0:T(8,128)S(1)} %fusion.103, bf16[512,24,5,128]{3,0,2,1:T(8,128)(2,1)} %get-tuple-element.209, s32[24,5]{0,1:T(8,128)S(1)} %get-tuple-element.233), kind=kOutput, calls=%fused_computation.12.clone.1 | convolution fusion | flops 190319424 | bytes 20447712 | tf_op jit(solution)/shard_map/while/body/eval_jaxpr/svob,voy->syb/dot_general | solution.py:59
  623.0 3.3 copy.125
  627.5 15.2 %fusion.102 = (bf16[512,24,5,128]{3,0,2,1:T(8,128)(2,1)}, bf16[512,24,5,128]{3,0,2,1:T(8,128)(2,1)}) fusion(bf16[24,5,128,128]{3,2,1,0:T(8,128)(2,1)} %get-tuple-element.232, bf16[2,512,24,128]{3,1,2,0:T(8,128)(2,1)} %get-tuple-element.231, s32[]{:T(128)} %get-tuple-element.223), kind=kOutput, calls=%fused_computation.6.clone.1 | convolution fusion | flops 2044723200 | bytes 38535680 | tf_op jit(solution)/shard_map/while/body/eval_jaxpr/tpf,pcfk->tpck/dot_general | solution.py:54
  642.7 15.6 %fusion.103 = f32[512,128,12,1]{1,2,3,0:T(8,128)S(1)} fusion(bf16[512,24,5,128]{3,0,2,1:T(8,128)(2,1)} %get-tuple-element.208, s32[24,5]{0,1:T(8,128)S(1)} %get-tuple-element.233), kind=kOutput, calls=%fused_computation.7.clone.1 | convolution fusion | flops 188746560 | bytes 18874848 | tf_op jit(solution)/shard_map/while/body/eval_jaxpr/svob,voy->syb/dot_general | solution.py:62
  658.4 15.6 %fusion.104 = bf16[512,12,128]{2,1,0:T(8,128)(2,1)} fusion(f32[512,128,12,1]{1,2,3,0:T(8,128)S(1)} %fusion.103, bf16[512,24,5,128]{3,0,2,1:T(8,128)(2,1)} %get-tuple-element.209, s32[24,5]{0,1:T(8,128)S(1)} %get-tuple-element.233), kind=kOutput, calls=%fused_computation.12.clone.1 | convolution fusion | flops 190319424 | bytes 20447712 | tf_op jit(solution)/shard_map/while/body/eval_jaxpr/svob,voy->syb/dot_general | solution.py:59
  678.7 4.7 copy.66
  683.4 18.7 %select_bitcast_fusion = f32[24,5,128,128]{2,3,1,0:T(8,128)} fusion(pred[24,5]{1,0:T(8,128)(4,1)S(1)} %copy-done.3, bf16[1024,24,128,1]{0,2,3,1:T(8,128)(2,1)} %bitcast.172, bf16[24,5,1024,128]{2,3,1,0:T(8,128)(2,1)} %copy.72, pred[24,5]{1,0:T(8,128)(4,1)S(1)} %copy-done.5), kind=kOutput, calls=%fused_computation.58 | convolution fusion | flops 4044226560 | bytes 45613296 | tf_op jit(solution)/shard_map/tpf,tpck->pcfk/dot_general | solution.py:89
  702.2 9.1 %copy.79 = f32[24,5,128,128]{3,2,1,0:T(8,128)} copy(f32[24,5,128,128]{2,3,1,0:T(8,128)} %select_bitcast_fusion) | data formatting | bytes 15728640
  711.3 18.8 %broadcast_select_fusion.6 = f32[24,5,128,128]{3,2,1,0:T(8,128)} fusion(pred[24,5]{1,0:T(8,128)(4,1)S(1)} %copy-done.3, bf16[1024,24,128,1]{0,2,3,1:T(8,128)(2,1)} %bitcast.171, bf16[24,5,1024,128]{2,3,1,0:T(8,128)(2,1)} %copy.61, pred[24,5]{1,0:T(8,128)(4,1)S(1)} %copy-done.5), kind=kOutput, calls=%fused_computation.59 | convolution fusion | flops 4044226560 | bytes 45613296 | tf_op jit(solution)/shard_map/tpck,tpf->pckf/dot_general | solution.py:96
  730.1 30.0 %reduce-scatter.9.cloned.1.call-done = bf16[64,1536]{1,0:T(8,128)(2,1)} async-done(((bf16[1024,1536]{1,0:T(8,128)(2,1)}), bf16[64,1536]{1,0:T(8,128)(2,1)}) %reduce-scatter.9.cloned.1.call-update) | async-done | bytes 196624 | tf_op jit(solution)/shard_map/reduce_scatter | solution.py:70
  (47 shorter events, 22.6 us)
Async XLA Ops:
  11.8 4.7 copy-start
  11.8 5.0 copy-start.6
  11.8 43.0 %all-to-all-start = ((bf16[128,8,1536]{0,2,1:T(8,128)(2,1)}), bf16[128,8,1536]{0,2,1:T(8,128)(2,1)S(1)}, u32[]{:S(2)}, u32[]{:S(2)}) async-start(bf16[128,8,1536]{0,2,1:T(8,128)(2,1)} %bitcast.168), calls=%async_computation | async-start | bytes 6291456 | tf_op jit(solution)/shard_map/all_to_all | solution.py:23
  16.4 290.3 %reduce-scatter.13.cloned.1.call-start = ((), (), s32[]{:S(2)}) async-start(), calls=%async_computation.10 | async-start | bytes 7077888
  16.6 265.1 %copy-start.4 = (pred[24,5]{1,0:T(8,128)(4,1)}, pred[24,5]{1,0:T(8,128)(4,1)S(1)}, u32[]{:S(2)}) copy-start(pred[24,5]{1,0:T(8,128)(4,1)S(1)} %copy.56) | copy-start | bytes 364
  16.9 0.6 copy-start.2
  152.0 197.9 %reduce-scatter.15.cloned.1.call-start = ((), (), s32[]{:S(2)}) async-start(), calls=%async_computation.11 | async-start | bytes 7077888
  306.7 92.0 %all-gather.5.cloned.1.call-start = ((), (), s32[]{:S(2)}) async-start(), calls=%async_computation.8 | async-start | bytes 7077888 | tf_op jit(solution)/shard_map/all_gather | solution.py:46
  353.9 180.7 %all-gather.3.cloned.1.call-start = ((), (), s32[]{:S(2)}) async-start(), calls=%async_computation.6 | async-start | bytes 7077888 | tf_op jit(solution)/shard_map/all_gather | solution.py:46
  354.4 375.7 %reduce-scatter.11.cloned.1.call-start = ((), (), s32[]{:S(2)}) async-start(), calls=%async_computation.9 | async-start | bytes 3342336 | tf_op jit(solution)/shard_map/reduce_scatter | solution.py:70
  409.8 18.2 %copy-start.1 = (s32[24,5]{0,1:T(8,128)S(1)}, s32[24,5]{0,1:T(8,128)}, u32[]{:S(2)}) copy-start(s32[24,5]{0,1:T(8,128)} %param.15) | copy-start | bytes 1444
  534.5 225.6 %reduce-scatter.9.cloned.1.call-start = ((), (), s32[]{:S(2)}) async-start(), calls=%async_computation.7 | async-start | bytes 3342336 | tf_op jit(solution)/shard_map/reduce_scatter | solution.py:70
  678.7 4.7 copy-start.3
  678.7 4.7 copy-start.5
Sparse Core Ops, SparseCore 0:
  152.1 74.9 reduce-scatter.12
  306.8 43.0 reduce-scatter.14
  354.0 44.6 all-gather.4
  400.2 45.9 all-gather.2
  534.6 76.5 reduce-scatter.10
  683.5 76.4 reduce-scatter.8
where the time goes:
time: 780 us; the launch traced here: 767 us
  local copies, waits for them, and re-layouts  265 us (34%)
  matrix products  256 us (33%)
  waiting for transfers between devices  148 us (19%)
  blocking collectives  57.4 us (7%)
  between operations  14.5 us (2%)
  loops' own time  13 us (2%)
  other arithmetic  8.03 us (1%)
    unnamed x23, local copies, waits for them, and re-layouts  70.7 us
    dot_general x4, matrix products, apply_block(): jnp.einsum('svob,voy->syb', lower_bound, block_selector, preferred_elemen...  62.8 us
    dot_general x4, matrix products, apply_block(): jnp.einsum('svob,voy->syb', upper_bound, block_selector, preferred_elemen...  62.6 us
    dot_general x4, matrix products, apply_block(): jnp.einsum(pattern, rows_block, weight_matrices, preferred_element_type=j...  60.3 us
    all_to_all x1, blocking collectives, on_device(): lax.all_to_all(upstream, 'narrow', split_axis=1, concat_axis=0, tiled=True)  57.4 us
    gather x2, local copies, waits for them, and re-layouts, on_device(): jnp.take(token_all.reshape(token_count, group_blocks, block_size), block_...  53 us
    gather x2, local copies, waits for them, and re-layouts, on_device(): jnp.take(upstream_all.reshape(token_count, group_blocks, block_size), blo...  53 us
    all_gather x2, waiting for transfers between devices, hidden_rows(): return lax.all_gather(share, 'narrow', axis=0, tiled=True)  44.2 us
  transfers between devices with their start and end apart: 7, of which 4 were waited for; matrix products, arithmetic and copies ran while one was open for 55% of the time, Pallas kernels for 0%

commit v1 on v0

v1 whole, which is shorter than its diff:
```python
import functools
import math

import jax
import jax.numpy as jnp
from jax import lax
from jax.experimental import pallas as pl
from jax.experimental.pallas import tpu as pltpu
from jax.sharding import PartitionSpec as P

MESH = pl.DeviceIdType.MESH
BLOCK = 128
PARTS = 4
ROWS = 64 // PARTS
VMEM_LIMIT = 62 * 1024 * 1024

Y_OF = ((0, 3, 1, 2), (0, 1, 3, 2))
SWAP = (0, 2, 1, 3, 4, 6, 5, 7)
PLANE = (
    (("x", 1), ("x", 3), ("z", 1), ("z", 3)),
    (("x", 3), ("x", 1), ("z", 3), ("z", 1)),
    (("z", 1), ("z", 3), ("x", 1), ("x", 3)),
    (("z", 3), ("z", 1), ("x", 3), ("x", 1)),
)


def flip(value, mask):
    if mask == 0:
        return value
    if mask == 1:
        return value + 1 - 2 * (value % 2)
    if mask == 2:
        return (value + 2) % 4
    return 3 - value


def place():
    wide, narrow = lax.axis_index("wide"), lax.axis_index("narrow")
    return wide // 4, wide % 4, narrow // 2, narrow % 2


def plane_partner(quarter, step, z, x):
    axis, mask = PLANE[quarter][3 - step]
    return (flip(z, mask), x) if axis == "z" else (z, flip(x, mask))


def plane_owner(quarter, position, z, x):
    masks = {"x": 0, "z": 0}
    for step in range(4):
        if position >> step & 1:
            axis, mask = PLANE[quarter][3 - step]
            masks[axis] ^= mask
    return flip(z, masks["z"]), flip(x, masks["x"])


def plane_position(quarter, z_bits, x_bits):
    total = 0
    for step in range(4):
        axis, mask = PLANE[quarter][3 - step]
        high, low = z_bits if axis == "z" else x_bits
        total = total + (high if mask == 3 else (high + low) % 2) * (1 << step)
    return total


def device(z, x, y, core):
    return (z * 4 + x, y * 2 + core)


def greet(partners):
    barrier = pltpu.get_barrier_semaphore()
    for partner in partners:
        pl.semaphore_signal(barrier, inc=1, device_id=partner, device_id_type=MESH)
    pl.semaphore_wait(barrier, len(partners))


def remote(src, dst, send, recv, target):
    return pltpu.make_async_remote_copy(
        src_ref=src, dst_ref=dst, send_sem=send, recv_sem=recv, device_id=target, device_id_type=MESH
    )


def gather_kernel(
    width, tok, up, xu, held, own_sem, sib_send, sib_recv, a_send, a_recv, g_send, g_recv, out_sem
):
    z, x, y, core = place()
    part = width // 4
    source, half = z // 2, z % 2
    sibling = device(z, x, y, 1 - core)
    slots = (1, 2, 3, 5, 6, 7)

    def peer(slot):
        yy = source * flip(y, Y_OF[0][slot % 4]) + (1 - source) * flip(y, Y_OF[1][slot % 4])
        return yy, (1 - core if slot >= 4 else core)

    peers = [peer(slot) for slot in slots]
    greet(
        [device(z, x, yy, cc) for yy, cc in peers]
        + [sibling]
        + [device(flip(z, 1), x, y, core), device(flip(z, 3), x, y, core)]
        + [device(z, flip(x, 1), y, core), device(z, flip(x, 3), y, core)]
    )

    def columns(yy, cc, start, size):
        return pl.ds(pl.multiple_of((yy * 2 + cc) * width + start, 128), size)

    first = []
    for s, (yy, cc) in enumerate(peers):
        cols = columns(yy, cc, x * part, part)

        def copy(ref, s=s, yy=yy, cc=cc, cols=cols):
            return remote(
                ref.at[half, :, :, cols], held.at[:, 0, s], a_send.at[s], a_recv.at[s], device(z, x, yy, cc)
            )

        @pl.when(source == 0)
        def _(copy=copy):
            copy(tok).start()

        @pl.when(source == 1)
        def _(copy=copy):
            copy(up).start()

        first.append(copy(tok))
    own, sib = [], []
    for a, ref in enumerate((tok, up)):
        for g in range(2):
            sib.append(
                remote(
                    ref.at[g, :, :, columns(y, 1 - core, 0, width)],
                    xu.at[a, :, 4, g],
                    sib_send.at[a, g],
                    sib_recv.at[a, g],
                    sibling,
                )
            )
            own.append(
                pltpu.make_async_copy(
                    ref.at[g, :, :, columns(y, core, 0, width)], xu.at[a, :, 0, g], own_sem.at[a, g]
                )
            )
    for copy in first:
        copy.wait()
    for copy in sib + own:
        copy.start()

    def spread(t, position):
        zz, xx = plane_owner(t % 4, position, z, x)
        cols = pl.ds(pl.multiple_of(xx * part, 128), part)
        for b in range(2):
            pltpu.make_async_copy(
                held.at[t, position, pl.ds(3 * b, 3)],
                xu.at[zz // 2, t, pl.ds(1 + 4 * b, 3), zz % 2, :, cols],
                out_sem,
            ).start()

    for step in range(4):
        size = 1 << step
        copies = []
        for t in range(PARTS):
            zz, xx = plane_partner(t % 4, step, z, x)
            copies.append(
                remote(
                    held.at[t, pl.ds(0, size)],
                    held.at[t, pl.ds(size, size)],
                    g_send.at[step, t],
                    g_recv.at[step, t],
                    device(zz, xx, y, core),
                )
            )
            copies[-1].start()
        for t in range(PARTS):
            for position in range(size // 2, size):
                spread(t, position)
        for copy in copies:
            copy.wait()
    for t in range(PARTS):
        for position in range(8, 16):
            spread(t, position)
    for copy in sib + own:
        copy.wait()
    pltpu.make_async_copy(held, held, out_sem).wait()


def gather_inputs(tokens, upstream):
    rows, total = tokens.shape
    width = total // 8
    shape = (2, PARTS, rows // 2 // PARTS, total)
    dma = pltpu.SemaphoreType.DMA
    return pl.pallas_call(
        functools.partial(gather_kernel, width),
        out_shape=jax.ShapeDtypeStruct((2, PARTS, 8, 2, ROWS, width), jnp.bfloat16),
        in_specs=[pl.BlockSpec(memory_space=pl.ANY)] * 2,
        out_specs=pl.BlockSpec(memory_space=pl.ANY),
        scratch_shapes=[
            pltpu.VMEM((PARTS, 16, 6, ROWS, width // 4), jnp.bfloat16),
            dma((2, 2)),
            dma((2, 2)),
            dma((2, 2)),
            dma((6,)),
            dma((6,)),
            dma((4, PARTS)),
            dma((4, PARTS)),
            dma,
        ],
        compiler_params=pltpu.CompilerParams(
            collective_id=0, has_side_effects=True, vmem_limit_bytes=VMEM_LIMIT
        ),
    )(tokens.reshape(shape), upstream.reshape(shape))


def dense_kernel(rows, count, first, second, dense_first, dense_second):
    panel = pl.program_id(0)
    dense_first[...] = jnp.zeros_like(dense_first)
    dense_second[...] = jnp.zeros_like(dense_second)
    for slot in range(first.shape[1]):

        @pl.when(slot < count[panel, 0])
        def _(slot=slot):
            at = pl.ds(pl.multiple_of(rows[panel, slot] * BLOCK, BLOCK), BLOCK)
            dense_first[at, :] = first[0, slot]
            dense_second[:, at] = second[0, slot]


def dense_weights(first, second, rows, count, width):
    panels, cap = first.shape[:2]
    hidden = panels * BLOCK
    block = pl.BlockSpec((1, cap, BLOCK, BLOCK), lambda j, *_: (j, 0, 0, 0))
    return pl.pallas_call(
        dense_kernel,
        grid_spec=pltpu.PrefetchScalarGridSpec(
            num_scalar_prefetch=2,
            grid=(panels,),
            in_specs=[block, block],
            out_specs=[
                pl.BlockSpec((width, BLOCK), lambda j, *_: (0, j)),
                pl.BlockSpec((BLOCK, width), lambda j, *_: (j, 0)),
            ],
        ),
        out_shape=[
            jax.ShapeDtypeStruct((width, hidden), jnp.bfloat16),
            jax.ShapeDtypeStruct((hidden, width), jnp.bfloat16),
        ],
    )(rows, count, first, second)


def layer_kernel(
    width,
    hidden,
    xu_in,
    first_in,
    second_in,
    out,
    grad,
    acts,
    xu,
    first,
    second,
    part,
    got4,
    got2,
    got1,
    sum3,
    sum2,
    sum1,
    sum0,
    load_sem,
    y_send,
    y_recv,
    p_send,
    p_recv,
    acts_sem,
    free_sem,
):
    z, x, y, core = place()
    tile = 256
    third = width // 2 // tile
    loads = [
        pltpu.make_async_copy(src, dst, load_sem.at[i])
        for i, (src, dst) in enumerate(((xu_in, xu), (first_in, first), (second_in, second)))
    ]
    for copy in loads:
        copy.start()
    sibling = device(z, x, y, 1 - core)
    y_partner = [[device(z, x, flip(y, m), core) for m in (3, 1)], [device(z, x, flip(y, m), core) for m in (1, 3)]]
    greet(
        [sibling]
        + y_partner[0]
        + [device(flip(z, 1), x, y, core), device(flip(z, 3), x, y, core)]
        + [device(z, flip(x, 1), y, core), device(z, flip(x, 3), y, core)]
    )
    for copy in loads:
        copy.wait()
    chunk = 16 * ROWS

    def sums_copy(step, a, t):
        if step == 2:
            src, dst, to = part.at[a, t, pl.ds(4, 4)], got4.at[a, t], sibling
        elif step == 1:
            src, dst, to = part.at[a, t, pl.ds(2, 2)], got2.at[a, t], y_partner[a][1]
        else:
            src, dst, to = part.at[a, t, pl.ds(1, 1)], got1.at[a, t], y_partner[a][0]
        return remote(src, dst, y_send.at[step, a, t], y_recv.at[step, a, t], to)

    def back_copy(step, a, t):
        to = sibling if step == 2 else y_partner[a][step]
        size = 1 << step
        return remote(
            part.at[a, t, pl.ds(0, size)],
            part.at[a, t, pl.ds(size, size)],
            y_send.at[3 + step, a, t],
            y_recv.at[3 + step, a, t],
            to,
        )

    def sums_arrive(step, a, t):
        sums_copy(step, a, t).wait()
        to = sibling if step == 2 else y_partner[a][step]
        pl.semaphore_signal(free_sem.at[step, a, t], inc=1, device_id=to, device_id_type=MESH)

    def send_back(step, a, t):
        pl.semaphore_wait(free_sem.at[step, a, t], 1)
        back_copy(step, a, t).start()

    def plane_copy(step, a, q, t):
        rows = pl.ds(q * ROWS, ROWS)
        buffer = got4.at[a, t]
        if step == 3:
            src, dst = buffer.at[pl.ds(2, 2), rows, :], sum3.at[a, t, :, rows, :]
        elif step == 2:
            src, dst = buffer.at[pl.ds(1, 1), rows, :], sum2.at[a, t, :, rows, :]
        elif step == 1:
            src, dst = buffer.at[0, rows, pl.ds(width, width)], sum1.at[a, t, rows, :]
        else:
            src, dst = buffer.at[0, rows, pl.ds(width // 2, width // 2)], sum0.at[a, t, rows, :]
        zz, xx = plane_partner(a * 2 + q, step, z, x)
        return remote(
            src, dst, p_send.at[step, a, q, t], p_recv.at[step, a, q, t], device(zz, xx, y, core)
        )

    def up(t):
        for a in range(2):

            def body(j, _, a=a):
                cols = pl.ds(pl.multiple_of(j * tile, tile), tile)
                rows = xu[a, t].reshape(chunk, width)
                if a == 0:
                    value = jnp.dot(rows, first[:, cols], preferred_element_type=jnp.float32)
                else:
                    value = lax.dot_general(
                        rows, second[cols, :], (((1,), (1,)), ((), ())), preferred_element_type=jnp.float32
                    )
                value = value.astype(jnp.bfloat16).reshape(8, 2 * ROWS, tile)
                for i in range(8):
                    part[a, t, SWAP[i], :, cols] = value[i]
                return 0

            lax.fori_loop(0, hidden // tile, body, 0)
            sums_copy(2, a, t).start()

    def add_into(t, step):
        got = (got1, got2, got4)[step]
        size = 1 << step
        for a in range(2):
            sums_arrive(step, a, t)

            def body(j, _, a=a):
                cols = pl.ds(pl.multiple_of(j * tile, tile), tile)
                total = part[a, t, :size, :, cols].astype(jnp.float32) + got[a, t, :, :, cols].astype(jnp.float32)
                part[a, t, :size, :, cols] = total.astype(jnp.bfloat16)
                return 0

            lax.fori_loop(0, hidden // tile, body, 0)
            sums_copy(step - 1, a, t).start()

    def activate(t):
        for a in range(2):
            sums_arrive(0, a, t)

        def body(j, _):
            cols = pl.ds(pl.multiple_of(j * tile, tile), tile)

            def whole(a):
                return part[a, t, 0, :, cols].astype(jnp.float32) + got1[a, t, 0, :, cols].astype(jnp.float32)

            v, g = whole(0), whole(1)
            scale = math.sqrt(2 / math.pi)
            square = v * v
            th = jnp.tanh(scale * (v + 0.044715 * square * v))
            slope = 0.5 * (1 + th) + 0.5 * v * (1 - th * th) * (scale * (1 + 3 * 0.044715 * square))
            part[0, t, 0, :, cols] = (0.5 * v * (1 + th)).astype(jnp.bfloat16)
            part[1, t, 0, :, cols] = (g * slope).astype(jnp.bfloat16)
            return 0

        lax.fori_loop(0, hidden // tile, body, 0)
        for a in range(2):
            send_back(0, a, t)

    def forward(t, step):
        for a in range(2):
            back_copy(step - 1, a, t).wait()
            send_back(step, a, t)

    def down(t):
        for a in range(2):
            back_copy(2, a, t).wait()
            pltpu.make_async_copy(part.at[a, t], acts.at[a, t], acts_sem.at[a, t]).start()
            for q in range(2):
                spots = []
                for i in range(8):
                    yy = flip(y, Y_OF[a][i % 4])
                    cc = 1 - core if i >= 4 else core
                    z_bits = ((yy // 2 + z // 2) % 2, (yy + z) % 2)
                    for r in range(2):
                        x_bits = ((cc + x // 2) % 2, (r + x) % 2)
                        spots.append(plane_position(a * 2 + q, z_bits, x_bits))

                def body(j, _, a=a, q=q, spots=spots):
                    cols = pl.ds(pl.multiple_of((q * third + j) * tile, tile), tile)
                    rows = part[a, t].reshape(chunk, hidden)
                    if a == 0:
                        value = jnp.dot(rows, second[:, cols], preferred_element_type=jnp.float32)
                    else:
                        value = lax.dot_general(
                            rows, first[cols, :], (((1,), (1,)), ((), ())), preferred_element_type=jnp.float32
                        )
                    value = value.astype(jnp.bfloat16).reshape(16, ROWS, tile)
                    for i, spot in enumerate(spots):
                        at = pl.ds(pl.multiple_of((spot % 4) * (width // 2) + j * tile, tile), tile)
                        got4[a, t, spot // 4, pl.ds(q * ROWS, ROWS), at] = value[i]
                    return 0

                lax.fori_loop(0, third, body, 0)
                plane_copy(3, a, q, t).start()

    def plane_add(t, step):
        for a in range(2):
            for q in range(2):
                plane_copy(step, a, q, t).wait()
            cols = pl.ds(0, {3: hidden, 2: hidden, 1: width, 0: width // 2}[step])
            if step == 3:
                for i in range(2):
                    got4[a, t, i] = (
                        got4[a, t, i].astype(jnp.float32) + sum3[a, t, i].astype(jnp.float32)
                    ).astype(jnp.bfloat16)
            else:
                mine = got4[a, t, 0, :, cols].astype(jnp.float32)
                theirs = sum2[a, t, 0] if step == 2 else (sum1 if step == 1 else sum0)[a, t]
                total = (mine + theirs.astype(jnp.float32)).astype(jnp.bfloat16)
                if step:
                    got4[a, t, 0, :, cols] = total
                else:
                    for q in range(2):
                        (out, grad)[a][pl.ds(t * ROWS, ROWS), pl.ds(q * (width // 2), width // 2)] = total[
                            q * ROWS : (q + 1) * ROWS
                        ]
            if step:
                for q in range(2):
                    plane_copy(step - 1, a, q, t).start()

    stages = [
        up,
        lambda t: add_into(t, 2),
        lambda t: add_into(t, 1),
        activate,
        lambda t: forward(t, 1),
        lambda t: forward(t, 2),
        down,
        lambda t: plane_add(t, 3),
        lambda t: plane_add(t, 2),
        lambda t: plane_add(t, 1),
        lambda t: plane_add(t, 0),
    ]
    for wave in range(len(stages) + PARTS - 1):
        for t in range(PARTS):
            if 0 <= wave - t < len(stages):
                stages[wave - t](t)
    for t in range(PARTS):
        for a in range(2):
            pltpu.make_async_copy(part.at[a, t], acts.at[a, t], acts_sem.at[a, t]).wait()


def layer(xu, first, second):
    width, hidden = first.shape
    dma = pltpu.SemaphoreType.DMA

    def vmem(*shape):
        return pltpu.VMEM(shape, jnp.bfloat16)

    pair, rows = (2, PARTS), 2 * ROWS
    whole = jax.ShapeDtypeStruct((64, width), jnp.bfloat16)
    return pl.pallas_call(
        functools.partial(layer_kernel, width, hidden),
        out_shape=[whole, whole, jax.ShapeDtypeStruct((*pair, 8, rows, hidden), jnp.bfloat16)],
        in_specs=[pl.BlockSpec(memory_space=pl.ANY)] * 3,
        out_specs=[
            pl.BlockSpec(memory_space=pltpu.VMEM),
            pl.BlockSpec(memory_space=pltpu.VMEM),
            pl.BlockSpec(memory_space=pl.ANY),
        ],
        scratch_shapes=[
            vmem(*xu.shape),
            vmem(*first.shape),
            vmem(*second.shape),
            vmem(*pair, 8, rows, hidden),
            vmem(*pair, 4, rows, hidden),
            vmem(*pair, 2, rows, hidden),
            vmem(*pair, 1, rows, hidden),
            vmem(*pair, 2, rows, hidden),
            vmem(*pair, 1, rows, hidden),
            vmem(*pair, rows, width),
            vmem(*pair, rows, width // 2),
            dma((3,)),
            dma((6, *pair)),
            dma((6, *pair)),
            dma((4, 2, 2, PARTS)),
            dma((4, 2, 2, PARTS)),
            dma(pair),
            pltpu.SemaphoreType.REGULAR((3, *pair)),
        ],
        compiler_params=pltpu.CompilerParams(
            collective_id=1, has_side_effects=True, vmem_limit_bytes=VMEM_LIMIT
        ),
    )(xu, first, second)


def grads_kernel(rows, count, xu, acts, first_grad, second_grad):
    panel = pl.program_id(0)
    hidden_turned = acts[0].T
    grad_turned = acts[1].T
    for slot in range(first_grad.shape[1]):
        kept = slot < count[panel, 0]

        @pl.when(kept)
        def _(slot=slot):
            at = pl.ds(pl.multiple_of(rows[panel, slot] * BLOCK, BLOCK), BLOCK)
            second_grad[0, slot] = jnp.dot(hidden_turned, xu[1, :, at], preferred_element_type=jnp.float32)
            first_grad[0, slot] = jnp.dot(grad_turned, xu[0, :, at], preferred_element_type=jnp.float32).T

        @pl.when(jnp.logical_not(kept))
        def _(slot=slot):
            second_grad[0, slot] = jnp.zeros((BLOCK, BLOCK), jnp.float32)
            first_grad[0, slot] = jnp.zeros((BLOCK, BLOCK), jnp.float32)


def weight_grads(xu, acts, rows, count):
    panels, cap = rows.shape
    tokens, width = math.prod(xu.shape[1:-1]), xu.shape[-1]
    block = pl.BlockSpec((1, cap, BLOCK, BLOCK), lambda j, *_: (j, 0, 0, 0))
    result = jax.ShapeDtypeStruct((panels, cap, BLOCK, BLOCK), jnp.float32)
    return pl.pallas_call(
        grads_kernel,
        grid_spec=pltpu.PrefetchScalarGridSpec(
            num_scalar_prefetch=2,
            grid=(panels,),
            in_specs=[
                pl.BlockSpec((2, tokens, width), lambda j, *_: (0, 0, 0)),
                pl.BlockSpec((2, tokens, BLOCK), lambda j, *_: (0, 0, j)),
            ],
            out_specs=[block, block],
        ),
        out_shape=[result, result],
        compiler_params=pltpu.CompilerParams(vmem_limit_bytes=VMEM_LIMIT),
    )(rows, count, xu.reshape(2, tokens, width), acts.reshape(2, tokens, panels * BLOCK))


def on_device(tokens, first_blocks, second_blocks, block_rows, block_count, upstream):
    width = tokens.shape[1] // lax.axis_size("narrow")
    first, second = dense_weights(first_blocks, second_blocks, block_rows, block_count, width)
    xu = gather_inputs(tokens, upstream)
    layer_output, grad_tokens, acts = layer(xu, first, second)
    first_grad, second_grad = weight_grads(xu, acts, block_rows, block_count)
    return layer_output, grad_tokens, first_grad, second_grad


def solution(mesh):
    blocks = P("wide", "narrow", None, None)
    return jax.shard_map(
        on_device,
        mesh=mesh,
        in_specs=(P("narrow", None), blocks, blocks, P("wide", "narrow"), P("wide", "narrow"), P("narrow", None)),
        out_specs=(P("wide", "narrow"), P("wide", "narrow"), blocks, blocks),
        check_vma=False,
    )
```

time: 780 us -> 279 us (0.36); the launches traced: 767 us -> 278 us
  Pallas kernels: 0 us -> 273 us
  local copies, waits for them, and re-layouts: 265 us -> 4.06 us
  matrix products: 256 us -> 0 us
  waiting for transfers between devices: 148 us -> 0 us
  blocking collectives: 57.4 us -> 0 us
  between operations: 14.5 us -> 0.67 us
  loops' own time: 13 us -> 0 us
  other arithmetic: 8.03 us -> 0 us
    pallas_call x0 -> x4, Pallas kernels: none -> 273 us  [the longest x1 162 us: layer(): pl.pallas_call(functools.partial(layer_kernel, width, hidden), out_shape=...]
    dot_general x16 -> x0, matrix products: 256 us -> none  [the longest x4 62.8 us: apply_block(): jnp.einsum('svob,voy->syb', lower_bound, block_selector, preferred_elemen...]
    gather x4 -> x0, local copies, waits for them, and re-layouts: 106 us -> none  [the longest x2 53 us: on_device(): jnp.take(token_all.reshape(token_count, group_blocks, block_size), block_...]
    unnamed x23 -> x8, local copies, waits for them, and re-layouts: 70.7 us -> 4.06 us
    all_to_all x1 -> x0, blocking collectives: 57.4 us -> none  [on_device(): lax.all_to_all(upstream, 'narrow', split_axis=1, concat_axis=0, tiled=True)]
    all_gather x2 -> x0, waiting for transfers between devices: 44.2 us -> none  [hidden_rows(): return lax.all_gather(share, 'narrow', axis=0, tiled=True)]
    unnamed x8 -> x0, waiting for transfers between devices: 42.3 us -> none
    all_to_all x1 -> x0, waiting for transfers between devices: 31.9 us -> none  [on_device(): lax.all_to_all(tokens, 'narrow', split_axis=1, concat_axis=0, tiled=True)]
  transfers between devices with their start and end apart: 7 -> 0, of which waited for: 4 -> 0; matrix products, arithmetic and copies ran while one was open for 55% -> 0% of each run, Pallas kernels for 0% -> 0%
where the time goes in v1:
time: 279 us; the launch traced here: 278 us
  Pallas kernels  273 us (98%)
  local copies, waits for them, and re-layouts  4.06 us (1%)
    pallas_call x1, Pallas kernels, layer(): pl.pallas_call(functools.partial(layer_kernel, width, hidden), out_shape=...  162 us
    pallas_call x1, Pallas kernels, gather_inputs(): pl.pallas_call(functools.partial(gather_kernel, width), out_shape=jax.Sha...  46.1 us
    pallas_call x1, Pallas kernels, weight_grads(): pl.pallas_call(grads_kernel, grid_spec=pltpu.PrefetchScalarGridSpec(num_s...  44.4 us
    pallas_call x1, Pallas kernels, dense_weights(): pl.pallas_call(dense_kernel, grid_spec=pltpu.PrefetchScalarGridSpec(num_s...  19.9 us

profile of v1, /device:TPU:2, one launch (start us, length us, event | category | flops | bytes accessed | tf_op | source)
XLA Modules:
  0.0 277.6 jit_solution(6200058419904595230)
XLA Ops:
  0.6 1.4 copy.10.rows
  2.0 1.3 copy.11.count
  3.3 46.1 %shard_map.93.xu_in = bf16[2,4,8,2,16,1536]{5,4,3,2,1,0:T(8,128)(2,1)} custom-call(bf16[2,4,16,12288]{3,2,1,0:T(8,128)(2,1)} %bitcast.6, bf16[2,4,16,12288]{3,2,1,0:T(8,128)(2,1)} %bitcast.7), custom_call_target="tpu_custom_call" | custom-call | tf_op jit(solution)/shard_map/pallas_call | solution.py:189
  49.5 19.9 %shard_map.94 = (bf16[1536,3072]{1,0:T(8,128)(2,1)}, bf16[3072,1536]{1,0:T(8,128)(2,1)}) custom-call(s32[24,5]{1,0:T(8,128)} %copy.10.rows, s32[24,1]{1,0:T(8,128)} %copy.11.count, bf16[24,5,128,128]{3,2,1,0:T(8,128)(2,1)} %first.1, bf16[24,5,128,128]{3,2,1,0:T(8,128)(2,1)} %second.1), custom_call_target="tpu_custom_call" | custom-call | tf_op jit(solution)/shard_map/pallas_call | solution.py:228
  69.3 162.5 %shard_map.95 = (bf16[64,1536]{1,0:T(8,128)(2,1)}, bf16[64,1536]{1,0:T(8,128)(2,1)}, bf16[2,4,8,32,3072]{4,3,2,1,0:T(8,128)(2,1)}) custom-call(bf16[2,4,8,2,16,1536]{5,4,3,2,1,0:T(8,128)(2,1)} %shard_map.93.xu_in, bf16[1536,3072]{1,0:T(8,128)(2,1)} %get-tuple-element.11.first_in, bf16[3072,1536]{1,0:T(8,128)(2,1)} %get-tuple-element.12.second_in), custom_call_target="tpu_custom_call" | custom-call | tf_op jit(solution)/shard_map/pallas_call | solution.py:491
  231.8 0.0 copy-start.1
  231.9 0.0 copy-start
  231.9 44.4 %shard_map.96 = (f32[24,5,128,128]{3,2,1,0:T(8,128)}, f32[24,5,128,128]{3,2,1,0:T(8,128)}) custom-call(s32[24,5]{1,0:T(8,128)} %copy.10.rows, s32[24,1]{1,0:T(8,128)} %copy.11.count, bf16[2,1024,1536]{2,1,0:T(8,128)(2,1)} %bitcast.4, bf16[2,1024,3072]{2,1,0:T(8,128)(2,1)} %bitcast.5), custom_call_target="tpu_custom_call" | custom-call | tf_op jit(solution)/shard_map/pallas_call | solution.py:550
  276.3 0.0 copy-done.1
  276.3 0.7 copy.16
  277.0 0.0 copy-done
  277.0 0.7 copy.17
Async XLA Ops:
  231.8 44.4 %copy-start.1 = (bf16[64,1536]{1,0:T(8,128)(2,1)S(1)}, bf16[64,1536]{1,0:T(8,128)(2,1)}, u32[]{:S(2)}) copy-start(bf16[64,1536]{1,0:T(8,128)(2,1)} %get-tuple-element.22) | copy-start | bytes 589828
  231.9 45.1 %copy-start = (bf16[64,1536]{1,0:T(8,128)(2,1)S(1)}, bf16[64,1536]{1,0:T(8,128)(2,1)}, u32[]{:S(2)}) copy-start(bf16[64,1536]{1,0:T(8,128)(2,1)} %get-tuple-element.23) | copy-start | bytes 589828

commit v2 on v1

v2 whole, which is shorter than its diff:
```python
import functools
import math

import jax
import jax.numpy as jnp
from jax import lax
from jax.experimental import pallas as pl
from jax.experimental.pallas import tpu as pltpu
from jax.sharding import PartitionSpec as P

MESH = pl.DeviceIdType.MESH
BLOCK = 128
PARTS = 4
ROWS = 64 // PARTS
GROUP = 4
VMEM_LIMIT = 62 * 1024 * 1024

Y_OF = ((0, 3, 1, 2), (0, 1, 3, 2))
SLOTS = (1, 2, 3, 5, 6, 7)
SWAP = (0, 2, 1, 3, 4, 6, 5, 7)
PLANE = (
    (("x", 1), ("x", 3), ("z", 1), ("z", 3)),
    (("x", 3), ("x", 1), ("z", 3), ("z", 1)),
    (("z", 1), ("z", 3), ("x", 1), ("x", 3)),
    (("z", 3), ("z", 1), ("x", 3), ("x", 1)),
)


def flip(value, mask):
    if mask == 0:
        return value
    if mask == 1:
        return value + 1 - 2 * (value % 2)
    if mask == 2:
        return (value + 2) % 4
    return 3 - value


def place():
    wide, narrow = lax.axis_index("wide"), lax.axis_index("narrow")
    return wide // 4, wide % 4, narrow // 2, narrow % 2


def plane_partner(quarter, step, z, x):
    axis, mask = PLANE[quarter][3 - step]
    return (flip(z, mask), x) if axis == "z" else (z, flip(x, mask))


def plane_owner(quarter, position, z, x):
    masks = {"x": 0, "z": 0}
    for step in range(4):
        if position >> step & 1:
            axis, mask = PLANE[quarter][3 - step]
            masks[axis] ^= mask
    return flip(z, masks["z"]), flip(x, masks["x"])


def plane_position(quarter, z_bits, x_bits):
    total = 0
    for step in range(4):
        axis, mask = PLANE[quarter][3 - step]
        high, low = z_bits if axis == "z" else x_bits
        total = total + (high if mask == 3 else (high + low) % 2) * (1 << step)
    return total


def device(z, x, y, core):
    return (z * 4 + x, y * 2 + core)


def greet(partners):
    barrier = pltpu.get_barrier_semaphore()
    for partner in partners:
        pl.semaphore_signal(barrier, inc=1, device_id=partner, device_id_type=MESH)
    pl.semaphore_wait(barrier, len(partners))


def remote(src, dst, send, recv, target):
    return pltpu.make_async_remote_copy(
        src_ref=src, dst_ref=dst, send_sem=send, recv_sem=recv, device_id=target, device_id_type=MESH
    )


def layer_kernel(
    width,
    hidden,
    cap,
    block_rows,
    block_count,
    tok,
    up_rows,
    first_in,
    second_in,
    out,
    grad,
    acts,
    xu_out,
    xu,
    first,
    second,
    raw_even,
    raw_odd,
    part,
    got4,
    got2,
    got1,
    sum3,
    sum2,
    sum1,
    sum0,
    load_sem,
    own_sem,
    sib_send,
    sib_recv,
    a_send,
    a_recv,
    g_send,
    g_recv,
    xu_sem,
    y_send,
    y_recv,
    p_send,
    p_recv,
    acts_sem,
    free_sem,
):
    z, x, y, core = place()
    tile = 256
    up_tile, down_tile = 512, width // 2
    chunk = 16 * ROWS
    piece = width // 4
    source, half = z // 2, z % 2
    sibling = device(z, x, y, 1 - core)
    y_partner = [[device(z, x, flip(y, m), core) for m in (3, 1)], [device(z, x, flip(y, m), core) for m in (1, 3)]]

    raw = (raw_even, raw_odd)

    def load(group):
        return [
            pltpu.make_async_copy(
                ref.at[pl.ds(group * GROUP, GROUP)],
                raw[group % 2].at[a, :, pl.ds(0, cap)],
                load_sem.at[a, group % 2],
            )
            for a, ref in enumerate((first_in, second_in))
        ]

    for group in range(2):
        for copy in load(group):
            copy.start()

    peers = []
    for slot in SLOTS:
        yy = source * flip(y, Y_OF[0][slot % 4]) + (1 - source) * flip(y, Y_OF[1][slot % 4])
        peers.append((yy, 1 - core if slot >= 4 else core))
    greet(
        [device(z, x, yy, cc) for yy, cc in peers]
        + [sibling]
        + [device(flip(z, 1), x, y, core), device(flip(z, 3), x, y, core)]
        + [device(z, flip(x, 1), y, core), device(z, flip(x, 3), y, core)]
    )

    def columns(yy, cc, start, size):
        return pl.ds(pl.multiple_of((yy * 2 + cc) * width + start, 128), size)

    first_copies = []
    for s, (yy, cc) in enumerate(peers):
        cols = columns(yy, cc, x * piece, piece)

        def copy(ref, s=s, yy=yy, cc=cc, cols=cols):
            return remote(
                ref.at[half, :, :, cols],
                part.at[0, :, 0, pl.ds(0, ROWS), pl.ds(s * piece, piece)],
                a_send.at[s],
                a_recv.at[s],
                device(z, x, yy, cc),
            )

        @pl.when(source == 0)
        def _(copy=copy):
            copy(tok).start()

        @pl.when(source == 1)
        def _(copy=copy):
            copy(up_rows).start()

        first_copies.append(copy(tok))
    near = []
    for a, ref in enumerate((tok, up_rows)):
        for g in range(2):
            near.append(
                remote(
                    ref.at[g, :, :, columns(y, 1 - core, 0, width)],
                    xu.at[a, :, 4, g],
                    sib_send.at[a, g],
                    sib_recv.at[a, g],
                    sibling,
                )
            )
            near.append(
                pltpu.make_async_copy(
                    ref.at[g, :, :, columns(y, core, 0, width)], xu.at[a, :, 0, g], own_sem.at[a, g]
                )
            )
    for copy in near:
        copy.start()
    for ref in raw:
        ref[:, :, cap] = jnp.zeros((2, GROUP, BLOCK, BLOCK), jnp.bfloat16)

    def place_blocks(group):
        for copy in load(group):
            copy.wait()

        def body(i, _):
            panel = group * GROUP + i
            across = pl.ds(pl.multiple_of(panel * BLOCK, BLOCK), BLOCK)
            for r in range(width // BLOCK):
                slot = cap
                for s in range(cap):
                    hit = jnp.logical_and(block_rows[panel, s] == r, s < block_count[panel, 0])
                    slot = jnp.where(hit, s, slot)
                first[r * BLOCK : (r + 1) * BLOCK, across] = raw[group % 2][0, i, slot]
                second[across, r * BLOCK : (r + 1) * BLOCK] = raw[group % 2][1, i, slot]
            return 0

        lax.fori_loop(0, GROUP, body, 0)
        if group + 2 < hidden // BLOCK // GROUP:
            for copy in load(group + 2):
                copy.start()

    def gather_copies(t, step):
        copies = []
        for u in range(3):
            cols = pl.ds(u * 2 * piece, 2 * piece)
            low, high = pl.ds(0, ROWS), pl.ds(ROWS, ROWS)
            if step == 0:
                src, dst = part.at[0, t, 0, low, cols], part.at[0, t, 0, high, cols]
            else:
                size = 1 << (step - 1)
                src = part.at[0, t, pl.ds(0, size), :, cols]
                dst = part.at[0, t, pl.ds(size, size), :, cols]
            zz, xx = plane_partner((t + u) % 4, step, z, x)
            copies.append(
                remote(src, dst, g_send.at[step, t, u], g_recv.at[step, t, u], device(zz, xx, y, core))
            )
        return copies

    def gather(t, step):
        if step == 0 and t == 0:
            for copy in first_copies:
                copy.wait()
        if step > 0:
            for copy in gather_copies(t, step - 1):
                copy.wait()
        for copy in gather_copies(t, step):
            copy.start()
        if t == 0 and step < 3:
            for group in range(2 * step, 2 * step + 2):
                place_blocks(group)

    def collect(t):
        for copy in gather_copies(t, 3):
            copy.wait()
        if t == 0:
            for copy in near:
                copy.wait()
        for u in range(3):
            for position in range(16):
                zz, xx = plane_owner((t + u) % 4, position, z, x)
                cols = pl.ds(pl.multiple_of(xx * piece, 128), piece)
                for s in (2 * u, 2 * u + 1):
                    xu[zz // 2, t, SLOTS[s], zz % 2, :, cols] = part[
                        0,
                        t,
                        position // 2,
                        (position % 2) * ROWS : (position % 2 + 1) * ROWS,
                        s * piece : (s + 1) * piece,
                    ]
        for a in range(2):
            pltpu.make_async_copy(xu.at[a, t], xu_out.at[a, t], xu_sem.at[a, t]).start()


    def sums_copy(step, a, t):
        if step == 2:
            src, dst, to = part.at[a, t, pl.ds(4, 4)], got4.at[a, t], sibling
        elif step == 1:
            src, dst, to = part.at[a, t, pl.ds(2, 2)], got2.at[a, t], y_partner[a][1]
        else:
            src, dst, to = part.at[a, t, pl.ds(1, 1)], got1.at[a, t], y_partner[a][0]
        return remote(src, dst, y_send.at[step, a, t], y_recv.at[step, a, t], to)

    def back_copy(step, a, t):
        to = sibling if step == 2 else y_partner[a][step]
        size = 1 << step
        return remote(
            part.at[a, t, pl.ds(0, size)],
            part.at[a, t, pl.ds(size, size)],
            y_send.at[3 + step, a, t],
            y_recv.at[3 + step, a, t],
            to,
        )

    def sums_arrive(step, a, t):
        sums_copy(step, a, t).wait()
        to = sibling if step == 2 else y_partner[a][step]
        pl.semaphore_signal(free_sem.at[step, a, t], inc=1, device_id=to, device_id_type=MESH)

    def send_back(step, a, t):
        pl.semaphore_wait(free_sem.at[step, a, t], 1)
        back_copy(step, a, t).start()

    def plane_copy(step, a, q, t):
        rows = pl.ds(q * ROWS, ROWS)
        buffer = got4.at[a, t]
        if step == 3:
            src, dst = buffer.at[pl.ds(2, 2), rows, :], sum3.at[a, t, :, rows, :]
        elif step == 2:
            src, dst = buffer.at[pl.ds(1, 1), rows, :], sum2.at[a, t, :, rows, :]
        elif step == 1:
            src, dst = buffer.at[0, rows, pl.ds(width, width)], sum1.at[a, t, rows, :]
        else:
            src, dst = buffer.at[0, rows, pl.ds(width // 2, width // 2)], sum0.at[a, t, rows, :]
        zz, xx = plane_partner(a * 2 + q, step, z, x)
        return remote(
            src, dst, p_send.at[step, a, q, t], p_recv.at[step, a, q, t], device(zz, xx, y, core)
        )

    def up(t):
        collect(t)
        for a in range(2):

            def body(j, _, a=a):
                cols = pl.ds(pl.multiple_of(j * up_tile, up_tile), up_tile)
                rows = xu[a, t].reshape(chunk, width)
                if a == 0:
                    value = jnp.dot(rows, first[:, cols], preferred_element_type=jnp.float32)
                else:
                    value = lax.dot_general(
                        rows, second[cols, :], (((1,), (1,)), ((), ())), preferred_element_type=jnp.float32
                    )
                value = value.astype(jnp.bfloat16).reshape(8, 2 * ROWS, up_tile)
                for i in range(8):
                    part[a, t, SWAP[i], :, cols] = value[i]
                return 0

            lax.fori_loop(0, hidden // up_tile, body, 0)
            sums_copy(2, a, t).start()

    def add_into(t, step):
        got = (got1, got2, got4)[step]
        size = 1 << step
        for a in range(2):
            sums_arrive(step, a, t)

            def body(j, _, a=a):
                cols = pl.ds(pl.multiple_of(j * tile, tile), tile)
                total = part[a, t, :size, :, cols].astype(jnp.float32) + got[a, t, :, :, cols].astype(jnp.float32)
                part[a, t, :size, :, cols] = total.astype(jnp.bfloat16)
                return 0

            lax.fori_loop(0, hidden // tile, body, 0)
            sums_copy(step - 1, a, t).start()

    def activate(t):
        for a in range(2):
            sums_arrive(0, a, t)

        def body(j, _):
            cols = pl.ds(pl.multiple_of(j * tile, tile), tile)

            def whole(a):
                return part[a, t, 0, :, cols].astype(jnp.float32) + got1[a, t, 0, :, cols].astype(jnp.float32)

            v, g = whole(0), whole(1)
            scale = math.sqrt(2 / math.pi)
            square = v * v
            th = jnp.tanh(scale * (v + 0.044715 * square * v))
            slope = 0.5 * (1 + th) + 0.5 * v * (1 - th * th) * (scale * (1 + 3 * 0.044715 * square))
            part[0, t, 0, :, cols] = (0.5 * v * (1 + th)).astype(jnp.bfloat16)
            part[1, t, 0, :, cols] = (g * slope).astype(jnp.bfloat16)
            return 0

        lax.fori_loop(0, hidden // tile, body, 0)
        for a in range(2):
            send_back(0, a, t)

    def forward(t, step):
        for a in range(2):
            back_copy(step - 1, a, t).wait()
            send_back(step, a, t)

    def down(t):
        for a in range(2):
            back_copy(2, a, t).wait()
            pltpu.make_async_copy(part.at[a, t], acts.at[a, t], acts_sem.at[a, t]).start()
            for q in range(2):
                spots = []
                for i in range(8):
                    yy = flip(y, Y_OF[a][i % 4])
                    cc = 1 - core if i >= 4 else core
                    z_bits = ((yy // 2 + z // 2) % 2, (yy + z) % 2)
                    for r in range(2):
                        x_bits = ((cc + x // 2) % 2, (r + x) % 2)
                        spots.append(plane_position(a * 2 + q, z_bits, x_bits))

                def body(a=a, q=q, spots=spots):
                    cols = pl.ds(pl.multiple_of(q * down_tile, down_tile), down_tile)
                    rows = part[a, t].reshape(chunk, hidden)
                    if a == 0:
                        value = jnp.dot(rows, second[:, cols], preferred_element_type=jnp.float32)
                    else:
                        value = lax.dot_general(
                            rows, first[cols, :], (((1,), (1,)), ((), ())), preferred_element_type=jnp.float32
                        )
                    value = value.astype(jnp.bfloat16).reshape(16, ROWS, down_tile)
                    for i, spot in enumerate(spots):
                        at = pl.ds(pl.multiple_of((spot % 4) * down_tile, down_tile), down_tile)
                        got4[a, t, spot // 4, pl.ds(q * ROWS, ROWS), at] = value[i]

                body()
                plane_copy(3, a, q, t).start()

    def plane_add(t, step):
        for a in range(2):
            for q in range(2):
                plane_copy(step, a, q, t).wait()
            cols = pl.ds(0, {3: hidden, 2: hidden, 1: width, 0: width // 2}[step])
            if step == 3:
                for i in range(2):
                    got4[a, t, i] = (
                        got4[a, t, i].astype(jnp.float32) + sum3[a, t, i].astype(jnp.float32)
                    ).astype(jnp.bfloat16)
            else:
                mine = got4[a, t, 0, :, cols].astype(jnp.float32)
                theirs = sum2[a, t, 0] if step == 2 else (sum1 if step == 1 else sum0)[a, t]
                total = (mine + theirs.astype(jnp.float32)).astype(jnp.bfloat16)
                if step:
                    got4[a, t, 0, :, cols] = total
                else:
                    for q in range(2):
                        (out, grad)[a][pl.ds(t * ROWS, ROWS), pl.ds(q * (width // 2), width // 2)] = total[
                            q * ROWS : (q + 1) * ROWS
                        ]
            if step:
                for q in range(2):
                    plane_copy(step - 1, a, q, t).start()

    stages = [
        lambda t: gather(t, 0),
        lambda t: gather(t, 1),
        lambda t: gather(t, 2),
        lambda t: gather(t, 3),
        up,
        lambda t: add_into(t, 2),
        lambda t: add_into(t, 1),
        activate,
        lambda t: forward(t, 1),
        lambda t: forward(t, 2),
        down,
        lambda t: plane_add(t, 3),
        lambda t: plane_add(t, 2),
        lambda t: plane_add(t, 1),
        lambda t: plane_add(t, 0),
    ]
    turn = [0, 0, 0, 0, 1, 0, 2, 2, 2, 2, 1, 2, 2, 2, 2]
    for wave in range(len(stages) + PARTS - 1):
        now = [t for t in range(PARTS) if 0 <= wave - t < len(stages)]
        for t in sorted(now, key=lambda t: (turn[wave - t], -t if wave - t > 4 else t)):
            stages[wave - t](t)
    for t in range(PARTS):
        for a in range(2):
            pltpu.make_async_copy(part.at[a, t], acts.at[a, t], acts_sem.at[a, t]).wait()
            pltpu.make_async_copy(xu.at[a, t], xu_out.at[a, t], xu_sem.at[a, t]).wait()


def layer(tokens, upstream, first_blocks, second_blocks, rows_of, count):
    local, total = tokens.shape
    panels, cap = first_blocks.shape[:2]
    width, hidden = total // 8, panels * BLOCK
    split = (2, PARTS, local // 2 // PARTS, total)
    dma = pltpu.SemaphoreType.DMA

    def vmem(*shape):
        return pltpu.VMEM(shape, jnp.bfloat16)

    pair, rows = (2, PARTS), 2 * ROWS
    inputs = (*pair, 8, 2, ROWS, width)
    whole = jax.ShapeDtypeStruct((64, width), jnp.bfloat16)
    anywhere = pl.BlockSpec(memory_space=pl.ANY)
    scalars = pl.BlockSpec(memory_space=pltpu.SMEM)
    on_chip = pl.BlockSpec(memory_space=pltpu.VMEM)
    return pl.pallas_call(
        functools.partial(layer_kernel, width, hidden, cap),
        out_shape=[
            whole,
            whole,
            jax.ShapeDtypeStruct((*pair, 8, rows, hidden), jnp.bfloat16),
            jax.ShapeDtypeStruct(inputs, jnp.bfloat16),
        ],
        in_specs=[scalars, scalars] + [anywhere] * 4,
        out_specs=[on_chip, on_chip, anywhere, anywhere],
        scratch_shapes=[
            vmem(*inputs),
            vmem(width, hidden),
            vmem(hidden, width),
            vmem(2, GROUP, cap + 1, BLOCK, BLOCK),
            vmem(2, GROUP, cap + 1, BLOCK, BLOCK),
            vmem(*pair, 8, rows, hidden),
            vmem(*pair, 4, rows, hidden),
            vmem(*pair, 2, rows, hidden),
            vmem(*pair, 1, rows, hidden),
            vmem(*pair, 2, rows, hidden),
            vmem(*pair, 1, rows, hidden),
            vmem(*pair, rows, width),
            vmem(*pair, rows, width // 2),
            dma((2, 2)),
            dma((2, 2)),
            dma((2, 2)),
            dma((2, 2)),
            dma((6,)),
            dma((6,)),
            dma((4, PARTS, 3)),
            dma((4, PARTS, 3)),
            dma(pair),
            dma((6, *pair)),
            dma((6, *pair)),
            dma((4, 2, 2, PARTS)),
            dma((4, 2, 2, PARTS)),
            dma(pair),
            pltpu.SemaphoreType.REGULAR((3, *pair)),
        ],
        compiler_params=pltpu.CompilerParams(
            collective_id=1, has_side_effects=True, vmem_limit_bytes=VMEM_LIMIT
        ),
    )(rows_of, count, tokens.reshape(split), upstream.reshape(split), first_blocks, second_blocks)


def grads_kernel(rows, count, xu, acts, first_grad, second_grad, turned):
    panel = pl.program_id(0)
    cap = first_grad.shape[1]

    @pl.when(panel == 0)
    def _():
        def body(r, _):
            at = pl.ds(pl.multiple_of(r * BLOCK, BLOCK), BLOCK)
            for a in range(2):
                turned[a, at, :] = xu[a, :, at].T
            return 0

        lax.fori_loop(0, xu.shape[2] // BLOCK, body, 0)

    def one(p, _):
        at_panel = pl.ds(pl.multiple_of(p * BLOCK, BLOCK), BLOCK)
        index = panel * first_grad.shape[0] + p
        for kept in range(1, cap + 1):

            @pl.when(count[index, 0] == kept)
            def _(kept=kept):
                for a, grad in ((0, first_grad), (1, second_grad)):
                    blocks = [
                        turned[a, pl.ds(pl.multiple_of(rows[index, slot] * BLOCK, BLOCK), BLOCK), :]
                        for slot in range(kept)
                    ]
                    value = jnp.dot(
                        jnp.concatenate(blocks), acts[1 - a, :, at_panel], preferred_element_type=jnp.float32
                    )
                    for slot in range(cap):
                        if slot >= kept:
                            grad[p, slot] = jnp.zeros((BLOCK, BLOCK), jnp.float32)
                        else:
                            block = value[slot * BLOCK : (slot + 1) * BLOCK]
                            grad[p, slot] = block.T if a else block

        return 0

    lax.fori_loop(0, first_grad.shape[0], one, 0)


def weight_grads(xu, acts, rows, count):
    panels, cap = rows.shape
    tokens, width = math.prod(xu.shape[1:-1]), xu.shape[-1]
    block = pl.BlockSpec((GROUP, cap, BLOCK, BLOCK), lambda j, *_: (j, 0, 0, 0))
    result = jax.ShapeDtypeStruct((panels, cap, BLOCK, BLOCK), jnp.float32)
    return pl.pallas_call(
        grads_kernel,
        grid_spec=pltpu.PrefetchScalarGridSpec(
            num_scalar_prefetch=2,
            grid=(panels // GROUP,),
            in_specs=[
                pl.BlockSpec((2, tokens, width), lambda j, *_: (0, 0, 0)),
                pl.BlockSpec((2, tokens, GROUP * BLOCK), lambda j, *_: (0, 0, j)),
            ],
            out_specs=[block, block],
            scratch_shapes=[pltpu.VMEM((2, width, tokens), jnp.bfloat16)],
        ),
        out_shape=[result, result],
        compiler_params=pltpu.CompilerParams(vmem_limit_bytes=VMEM_LIMIT),
    )(rows, count, xu.reshape(2, tokens, width), acts.reshape(2, tokens, panels * BLOCK))


def on_device(tokens, first_blocks, second_blocks, block_rows, block_count, upstream):
    layer_output, grad_tokens, acts, xu = layer(
        tokens, upstream, first_blocks, second_blocks, block_rows, block_count
    )
    first_grad, second_grad = weight_grads(xu, acts, block_rows, block_count)
    return layer_output, grad_tokens, first_grad, second_grad


def solution(mesh):
    blocks = P("wide", "narrow", None, None)
    return jax.shard_map(
        on_device,
        mesh=mesh,
        in_specs=(P("narrow", None), blocks, blocks, P("wide", "narrow"), P("wide", "narrow"), P("narrow", None)),
        out_specs=(P("wide", "narrow"), P("wide", "narrow"), blocks, blocks),
        check_vma=False,
    )
```

time: 279 us -> 213 us (0.76)
  Pallas kernels: 273 us -> 207 us
    pallas_call x3 -> x1, Pallas kernels: 228 us -> 182 us  [layer(): pl.pallas_call(functools.partial(layer_kernel, width, hidden, cap), out_s...]
    pallas_call x1, Pallas kernels: 44.4 us -> 24.9 us  [weight_grads(): pl.pallas_call(grads_kernel, grid_spec=pltpu.PrefetchScalarGridSpec(num_s...]
where the time goes in v2:
time: 213 us; the launch traced here: 211 us
  Pallas kernels  207 us (97%)
  local copies, waits for them, and re-layouts  4.06 us (2%)
    pallas_call x1, Pallas kernels, layer(): pl.pallas_call(functools.partial(layer_kernel, width, hidden, cap), out_s...  182 us
    pallas_call x1, Pallas kernels, weight_grads(): pl.pallas_call(grads_kernel, grid_spec=pltpu.PrefetchScalarGridSpec(num_s...  24.9 us

profile of v2, /device:TPU:2, one launch (start us, length us, event | category | flops | bytes accessed | tf_op | source)
XLA Modules:
  0.0 211.3 jit_solution(18071468950868609629)
XLA Ops:
  0.6 1.4 copy.10.block_rows.rows
  2.0 1.3 copy.11.block_count.count
  3.3 181.7 %shard_map.93 = (bf16[64,1536]{1,0:T(8,128)(2,1)}, bf16[64,1536]{1,0:T(8,128)(2,1)}, bf16[2,4,8,32,3072]{4,3,2,1,0:T(8,128)(2,1)}, bf16[2,4,8,2,16,1536]{5,4,3,2,1,0:T(8,128)(2,1)}) custom-call(s32[24,5]{1,0:T(8,128)} %copy.10.block_rows.rows, s32[24,1]{1,0:T(8,128)} %copy.11.block_count.count, bf16[2,4,16,12288]{3,2,1,0:T(8,128)(2,1)} %bitcast.6, ...), custom_call_target="tpu_custom_call" | custom-call | tf_op jit(solution)/shard_map/pallas_call | solution.py:492
  185.0 0.0 copy-start.1
  185.0 0.0 copy-start
  185.0 24.9 %shard_map.94 = (f32[24,5,128,128]{3,2,1,0:T(8,128)}, f32[24,5,128,128]{3,2,1,0:T(8,128)}) custom-call(s32[24,5]{1,0:T(8,128)} %copy.10.block_rows.rows, s32[24,1]{1,0:T(8,128)} %copy.11.block_count.count, bf16[2,1024,1536]{2,1,0:T(8,128)(2,1)} %bitcast.5, bf16[2,1024,3072]{2,1,0:T(8,128)(2,1)} %bitcast.4), custom_call_target="tpu_custom_call" | custom-call | tf_op jit(solution)/shard_map/pallas_call | solution.py:584
  209.9 0.0 copy-done.1
  209.9 0.7 copy.16
  210.6 0.0 copy-done
  210.6 0.7 copy.17
Async XLA Ops:
  185.0 24.9 %copy-start.1 = (bf16[64,1536]{1,0:T(8,128)(2,1)S(1)}, bf16[64,1536]{1,0:T(8,128)(2,1)}, u32[]{:S(2)}) copy-start(bf16[64,1536]{1,0:T(8,128)(2,1)} %get-tuple-element.20) | copy-start | bytes 589828
  185.0 25.6 %copy-start = (bf16[64,1536]{1,0:T(8,128)(2,1)S(1)}, bf16[64,1536]{1,0:T(8,128)(2,1)}, u32[]{:S(2)}) copy-start(bf16[64,1536]{1,0:T(8,128)(2,1)} %get-tuple-element.21) | copy-start | bytes 589828

commit v3 on v2

--- a/solution.py
+++ b/solution.py
@@ -23,6 +23,28 @@
     (("x", 3), ("x", 1), ("z", 3), ("z", 1)),
     (("z", 1), ("z", 3), ("x", 1), ("x", 3)),
     (("z", 3), ("z", 1), ("x", 3), ("x", 1)),
+)
+
+ORDER = (
+    ("dens", 0, 0), ("dens", 1, 0), ("g0", 0, 0), ("g0", 1, 0), ("g1", 0, 0), ("g1", 1, 0),
+    ("g0", 2, 0), ("g2", 0, 0), ("dens", 2, 0), ("g3", 0, 0), ("dens", 3, 0), ("dens", 4, 0),
+    ("dens", 5, 0), ("g1", 2, 0), ("g2", 1, 0), ("col", 0, 0), ("up", 0, 1), ("g3", 1, 0),
+    ("up", 0, 0), ("s1", 0, 1), ("g0", 3, 0), ("s1", 0, 0), ("g2", 2, 0), ("col", 1, 0),
+    ("up", 1, 1), ("up", 1, 0), ("s1", 1, 1), ("s2", 0, 1), ("g3", 2, 0), ("s2", 0, 0),
+    ("s1", 1, 0), ("col", 2, 0), ("g1", 3, 0), ("up", 2, 1), ("act", 0, 0), ("s2", 1, 1),
+    ("g2", 3, 0), ("s1", 2, 1), ("up", 2, 0), ("f1", 0, 1), ("s1", 2, 0), ("g3", 3, 0),
+    ("s2", 2, 1), ("f1", 0, 0), ("col", 3, 0), ("s2", 2, 0), ("up", 3, 1), ("f2", 0, 1),
+    ("s2", 1, 0), ("up", 3, 0), ("s1", 3, 1), ("act", 2, 0), ("s1", 3, 0), ("f2", 0, 0),
+    ("f1", 2, 1), ("f1", 2, 0), ("d", 0, 0), ("d", 0, 1), ("act", 1, 0), ("p3", 0, 1),
+    ("s2", 3, 0), ("s2", 3, 1), ("f2", 2, 1), ("p2", 0, 1), ("p3", 0, 0), ("f1", 1, 1),
+    ("f2", 2, 0), ("f1", 1, 0), ("d", 2, 1), ("d", 2, 0), ("p1", 0, 1), ("p2", 0, 0),
+    ("act", 3, 0), ("f2", 1, 1), ("p3", 2, 1), ("f2", 1, 0), ("p3", 2, 0), ("f1", 3, 0),
+    ("d", 1, 1), ("f1", 3, 1), ("d", 1, 0), ("f2", 3, 0), ("p1", 0, 0), ("p2", 2, 0),
+    ("p3", 1, 1), ("p3", 1, 0), ("f2", 3, 1), ("d", 3, 0), ("p2", 1, 0), ("d", 3, 1),
+    ("p2", 2, 1), ("p2", 1, 1), ("p1", 2, 1), ("p1", 2, 0), ("p1", 1, 0), ("p3", 3, 0),
+    ("p3", 3, 1), ("p0", 1, 0), ("p0", 0, 0), ("p0", 2, 1), ("p1", 1, 1), ("p2", 3, 0),
+    ("p2", 3, 1), ("p1", 3, 0), ("p1", 3, 1), ("p0", 0, 1), ("p0", 2, 0), ("p0", 1, 1),
+    ("p0", 3, 0), ("p0", 3, 1),
 )
 
 
@@ -94,13 +116,14 @@
     out,
     grad,
     acts,
-    xu_out,
+    xt,
     xu,
     first,
     second,
     raw_even,
     raw_odd,
     part,
+    turned,
     got4,
     got2,
     got1,
@@ -116,7 +139,7 @@
     a_recv,
     g_send,
     g_recv,
-    xu_sem,
+    xt_sem,
     y_send,
     y_recv,
     p_send,
@@ -163,28 +186,29 @@
     def columns(yy, cc, start, size):
         return pl.ds(pl.multiple_of((yy * 2 + cc) * width + start, 128), size)
 
-    first_copies = []
-    for s, (yy, cc) in enumerate(peers):
-        cols = columns(yy, cc, x * piece, piece)
-
-        def copy(ref, s=s, yy=yy, cc=cc, cols=cols):
-            return remote(
-                ref.at[half, :, :, cols],
-                part.at[0, :, 0, pl.ds(0, ROWS), pl.ds(s * piece, piece)],
-                a_send.at[s],
-                a_recv.at[s],
-                device(z, x, yy, cc),
-            )
-
-        @pl.when(source == 0)
-        def _(copy=copy):
-            copy(tok).start()
-
-        @pl.when(source == 1)
-        def _(copy=copy):
-            copy(up_rows).start()
-
-        first_copies.append(copy(tok))
+    first_copies = [[] for _ in range(PARTS)]
+    for t in range(PARTS):
+        for s, (yy, cc) in enumerate(peers):
+            cols = columns(yy, cc, x * piece, piece)
+
+            def copy(ref, t=t, s=s, yy=yy, cc=cc, cols=cols):
+                return remote(
+                    ref.at[half, t, :, cols],
+                    part.at[0, t, 0, pl.ds(0, ROWS), pl.ds(s * piece, piece)],
+                    a_send.at[s, t],
+                    a_recv.at[s, t],
+                    device(z, x, yy, cc),
+                )
+
+            @pl.when(source == 0)
+            def _(copy=copy):
+                copy(tok).start()
+
+            @pl.when(source == 1)
+            def _(copy=copy):
+                copy(up_rows).start()
+
+            first_copies[t].append(copy(tok))
     near = []
     for a, ref in enumerate((tok, up_rows)):
         for g in range(2):
@@ -217,7 +241,7 @@
             for r in range(width // BLOCK):
                 slot = cap
                 for s in range(cap):
-                    hit = jnp.logical_and(block_rows[panel, s] == r, s < block_count[panel, 0])
+                    hit = jnp.logical_and(block_rows[s, panel] == r, s < block_count[panel])
                     slot = jnp.where(hit, s, slot)
                 first[r * BLOCK : (r + 1) * BLOCK, across] = raw[group % 2][0, i, slot]
                 second[across, r * BLOCK : (r + 1) * BLOCK] = raw[group % 2][1, i, slot]
@@ -246,24 +270,20 @@
         return copies
 
     def gather(t, step):
-        if step == 0 and t == 0:
-            for copy in first_copies:
+        if step == 0:
+            for copy in first_copies[t]:
                 copy.wait()
         if step > 0:
             for copy in gather_copies(t, step - 1):
                 copy.wait()
         for copy in gather_copies(t, step):
             copy.start()
-        if t == 0 and step < 3:
-            for group in range(2 * step, 2 * step + 2):
-                place_blocks(group)
 
     def collect(t):
         for copy in gather_copies(t, 3):
             copy.wait()
-        if t == 0:
-            for copy in near:
-                copy.wait()
+        while near:
+            near.pop().wait()
         for u in range(3):
             for position in range(16):
                 zz, xx = plane_owner((t + u) % 4, position, z, x)
@@ -276,9 +296,21 @@
                         (position % 2) * ROWS : (position % 2 + 1) * ROWS,
                         s * piece : (s + 1) * piece,
                     ]
+
+    turning = []
+
+    def turn_copies(t):
+        cols = pl.ds(t * chunk, chunk)
+        return [pltpu.make_async_copy(turned.at[a], xt.at[a, :, cols], xt_sem.at[a]) for a in range(2)]
+
+    def turn_inputs(t):
+        while turning:
+            turning.pop().wait()
         for a in range(2):
-            pltpu.make_async_copy(xu.at[a, t], xu_out.at[a, t], xu_sem.at[a, t]).start()
-
+            turned[a] = xu[a, t].reshape(chunk, width).T
+        for copy in turn_copies(t):
+            copy.start()
+            turning.append(copy)
 
     def sums_copy(step, a, t):
         if step == 2:
@@ -325,41 +357,38 @@
             src, dst, p_send.at[step, a, q, t], p_recv.at[step, a, q, t], device(zz, xx, y, core)
         )
 
-    def up(t):
-        collect(t)
-        for a in range(2):
-
-            def body(j, _, a=a):
-                cols = pl.ds(pl.multiple_of(j * up_tile, up_tile), up_tile)
-                rows = xu[a, t].reshape(chunk, width)
-                if a == 0:
-                    value = jnp.dot(rows, first[:, cols], preferred_element_type=jnp.float32)
-                else:
-                    value = lax.dot_general(
-                        rows, second[cols, :], (((1,), (1,)), ((), ())), preferred_element_type=jnp.float32
-                    )
-                value = value.astype(jnp.bfloat16).reshape(8, 2 * ROWS, up_tile)
-                for i in range(8):
-                    part[a, t, SWAP[i], :, cols] = value[i]
-                return 0
-
-            lax.fori_loop(0, hidden // up_tile, body, 0)
-            sums_copy(2, a, t).start()
-
-    def add_into(t, step):
+    def up(t, a):
+
+        def body(j, _, a=a):
+            cols = pl.ds(pl.multiple_of(j * up_tile, up_tile), up_tile)
+            rows = xu[a, t].reshape(chunk, width)
+            if a == 0:
+                value = jnp.dot(rows, first[:, cols], preferred_element_type=jnp.float32)
+            else:
+                value = lax.dot_general(
+                    rows, second[cols, :], (((1,), (1,)), ((), ())), preferred_element_type=jnp.float32
+                )
+            value = value.astype(jnp.bfloat16).reshape(8, 2 * ROWS, up_tile)
+            for i in range(8):
+                part[a, t, SWAP[i], :, cols] = value[i]
+            return 0
+
+        lax.fori_loop(0, hidden // up_tile, body, 0)
+        sums_copy(2, a, t).start()
+
+    def add_into(t, a, step):
         got = (got1, got2, got4)[step]
         size = 1 << step
-        for a in range(2):
-            sums_arrive(step, a, t)
-
-            def body(j, _, a=a):
-                cols = pl.ds(pl.multiple_of(j * tile, tile), tile)
-                total = part[a, t, :size, :, cols].astype(jnp.float32) + got[a, t, :, :, cols].astype(jnp.float32)
-                part[a, t, :size, :, cols] = total.astype(jnp.bfloat16)
-                return 0
-
-            lax.fori_loop(0, hidden // tile, body, 0)
-            sums_copy(step - 1, a, t).start()
+        sums_arrive(step, a, t)
+
+        def body(j, _, a=a):
+            cols = pl.ds(pl.multiple_of(j * tile, tile), tile)
+            total = part[a, t, :size, :, cols].astype(jnp.float32) + got[a, t, :, :, cols].astype(jnp.float32)
+            part[a, t, :size, :, cols] = total.astype(jnp.bfloat16)
+            return 0
+
+        lax.fori_loop(0, hidden // tile, body, 0)
+        sums_copy(step - 1, a, t).start()
 
     def activate(t):
         for a in range(2):
@@ -383,94 +412,87 @@
         lax.fori_loop(0, hidden // tile, body, 0)
         for a in range(2):
             send_back(0, a, t)
-
-    def forward(t, step):
-        for a in range(2):
-            back_copy(step - 1, a, t).wait()
-            send_back(step, a, t)
-
-    def down(t):
-        for a in range(2):
-            back_copy(2, a, t).wait()
-            pltpu.make_async_copy(part.at[a, t], acts.at[a, t], acts_sem.at[a, t]).start()
+        turn_inputs(t)
+
+    def forward(t, a, step):
+        back_copy(step - 1, a, t).wait()
+        send_back(step, a, t)
+
+    def down(t, a):
+        back_copy(2, a, t).wait()
+        pltpu.make_async_copy(part.at[a, t], acts.at[a, t], acts_sem.at[a, t]).start()
+        for q in range(2):
+            spots = []
+            for i in range(8):
+                yy = flip(y, Y_OF[a][i % 4])
+                cc = 1 - core if i >= 4 else core
+                z_bits = ((yy // 2 + z // 2) % 2, (yy + z) % 2)
+                for r in range(2):
+                    x_bits = ((cc + x // 2) % 2, (r + x) % 2)
+                    spots.append(plane_position(a * 2 + q, z_bits, x_bits))
+
+            def body(a=a, q=q, spots=spots):
+                cols = pl.ds(pl.multiple_of(q * down_tile, down_tile), down_tile)
+                rows = part[a, t].reshape(chunk, hidden)
+                if a == 0:
+                    value = jnp.dot(rows, second[:, cols], preferred_element_type=jnp.float32)
+                else:
+                    value = lax.dot_general(
+                        rows, first[cols, :], (((1,), (1,)), ((), ())), preferred_element_type=jnp.float32
+                    )
+                value = value.astype(jnp.bfloat16).reshape(16, ROWS, down_tile)
+                for i, spot in enumerate(spots):
+                    at = pl.ds(pl.multiple_of((spot % 4) * down_tile, down_tile), down_tile)
+                    got4[a, t, spot // 4, pl.ds(q * ROWS, ROWS), at] = value[i]
+
+            body()
+            plane_copy(3, a, q, t).start()
+
+    def plane_add(t, a, step):
+        for q in range(2):
+            plane_copy(step, a, q, t).wait()
+        cols = pl.ds(0, {3: hidden, 2: hidden, 1: width, 0: width // 2}[step])
+        if step == 3:
+            for i in range(2):
+                got4[a, t, i] = (
+                    got4[a, t, i].astype(jnp.float32) + sum3[a, t, i].astype(jnp.float32)
+                ).astype(jnp.bfloat16)
+        else:
+            mine = got4[a, t, 0, :, cols].astype(jnp.float32)
+            theirs = sum2[a, t, 0] if step == 2 else (sum1 if step == 1 else sum0)[a, t]
+            total = (mine + theirs.astype(jnp.float32)).astype(jnp.bfloat16)
+            if step:
+                got4[a, t, 0, :, cols] = total
+            else:
+                for q in range(2):
+                    (out, grad)[a][pl.ds(t * ROWS, ROWS), pl.ds(q * (width // 2), width // 2)] = total[
+                        q * ROWS : (q + 1) * ROWS
+                    ]
+        if step:
             for q in range(2):
-                spots = []
-                for i in range(8):
-                    yy = flip(y, Y_OF[a][i % 4])
-                    cc = 1 - core if i >= 4 else core
-                    z_bits = ((yy // 2 + z // 2) % 2, (yy + z) % 2)
-                    for r in range(2):
-                        x_bits = ((cc + x // 2) % 2, (r + x) % 2)
-                        spots.append(plane_position(a * 2 + q, z_bits, x_bits))
-
-                def body(a=a, q=q, spots=spots):
-                    cols = pl.ds(pl.multiple_of(q * down_tile, down_tile), down_tile)
-                    rows = part[a, t].reshape(chunk, hidden)
-                    if a == 0:
-                        value = jnp.dot(rows, second[:, cols], preferred_element_type=jnp.float32)
-                    else:
-                        value = lax.dot_general(
-                            rows, first[cols, :], (((1,), (1,)), ((), ())), preferred_element_type=jnp.float32
-                        )
-                    value = value.astype(jnp.bfloat16).reshape(16, ROWS, down_tile)
-                    for i, spot in enumerate(spots):
-                        at = pl.ds(pl.multiple_of((spot % 4) * down_tile, down_tile), down_tile)
-                        got4[a, t, spot // 4, pl.ds(q * ROWS, ROWS), at] = value[i]
-
-                body()
-                plane_copy(3, a, q, t).start()
-
-    def plane_add(t, step):
-        for a in range(2):
-            for q in range(2):
-                plane_copy(step, a, q, t).wait()
-            cols = pl.ds(0, {3: hidden, 2: hidden, 1: width, 0: width // 2}[step])
-            if step == 3:
-                for i in range(2):
-                    got4[a, t, i] = (
-                        got4[a, t, i].astype(jnp.float32) + sum3[a, t, i].astype(jnp.float32)
-                    ).astype(jnp.bfloat16)
-            else:
-                mine = got4[a, t, 0, :, cols].astype(jnp.float32)
-                theirs = sum2[a, t, 0] if step == 2 else (sum1 if step == 1 else sum0)[a, t]
-                total = (mine + theirs.astype(jnp.float32)).astype(jnp.bfloat16)
-                if step:
-                    got4[a, t, 0, :, cols] = total
-                else:
-                    for q in range(2):
-                        (out, grad)[a][pl.ds(t * ROWS, ROWS), pl.ds(q * (width // 2), width // 2)] = total[
-                            q * ROWS : (q + 1) * ROWS
-                        ]
-            if step:
-                for q in range(2):
-                    plane_copy(step - 1, a, q, t).start()
-
-    stages = [
-        lambda t: gather(t, 0),
-        lambda t: gather(t, 1),
-        lambda t: gather(t, 2),
-        lambda t: gather(t, 3),
-        up,
-        lambda t: add_into(t, 2),
-        lambda t: add_into(t, 1),
-        activate,
-        lambda t: forward(t, 1),
-        lambda t: forward(t, 2),
-        down,
-        lambda t: plane_add(t, 3),
-        lambda t: plane_add(t, 2),
-        lambda t: plane_add(t, 1),
-        lambda t: plane_add(t, 0),
-    ]
-    turn = [0, 0, 0, 0, 1, 0, 2, 2, 2, 2, 1, 2, 2, 2, 2]
-    for wave in range(len(stages) + PARTS - 1):
-        now = [t for t in range(PARTS) if 0 <= wave - t < len(stages)]
-        for t in sorted(now, key=lambda t: (turn[wave - t], -t if wave - t > 4 else t)):
-            stages[wave - t](t)
+                plane_copy(step - 1, a, q, t).start()
+
+    stages = {
+        "up": up,
+        "s1": lambda t, a: add_into(t, a, 2),
+        "s2": lambda t, a: add_into(t, a, 1),
+        "act": lambda t, a: activate(t),
+        "f1": lambda t, a: forward(t, a, 1),
+        "f2": lambda t, a: forward(t, a, 2),
+        "d": down,
+        "dens": lambda group, a: place_blocks(group),
+        "col": lambda t, a: collect(t),
+    }
+    for step in range(4):
+        stages[f"g{step}"] = lambda t, a, step=step: gather(t, step)
+        stages[f"p{step}"] = lambda t, a, step=step: plane_add(t, a, step)
+    for name, t, a in ORDER:
+        stages[name](t, a)
     for t in range(PARTS):
         for a in range(2):
             pltpu.make_async_copy(part.at[a, t], acts.at[a, t], acts_sem.at[a, t]).wait()
-            pltpu.make_async_copy(xu.at[a, t], xu_out.at[a, t], xu_sem.at[a, t]).wait()
+    while turning:
+        turning.pop().wait()
 
 
 def layer(tokens, upstream, first_blocks, second_blocks, rows_of, count):
@@ -495,7 +517,7 @@
             whole,
             whole,
             jax.ShapeDtypeStruct((*pair, 8, rows, hidden), jnp.bfloat16),
-            jax.ShapeDtypeStruct(inputs, jnp.bfloat16),
+            jax.ShapeDtypeStruct((2, width, 16 * ROWS * PARTS), jnp.bfloat16),
         ],
         in_specs=[scalars, scalars] + [anywhere] * 4,
         out_specs=[on_chip, on_chip, anywhere, anywhere],
@@ -506,6 +528,7 @@
             vmem(2, GROUP, cap + 1, BLOCK, BLOCK),
             vmem(2, GROUP, cap + 1, BLOCK, BLOCK),
             vmem(*pair, 8, rows, hidden),
+            vmem(2, width, 16 * ROWS),
             vmem(*pair, 4, rows, hidden),
             vmem(*pair, 2, rows, hidden),
             vmem(*pair, 1, rows, hidden),
@@ -517,11 +540,11 @@
             dma((2, 2)),
             dma((2, 2)),
             dma((2, 2)),
-            dma((6,)),
-            dma((6,)),
+            dma((6, PARTS)),
+            dma((6, PARTS)),
             dma((4, PARTS, 3)),
             dma((4, PARTS, 3)),
-            dma(pair),
+            dma((2,)),
             dma((6, *pair)),
             dma((6, *pair)),
             dma((4, 2, 2, PARTS)),
@@ -535,30 +558,20 @@
     )(rows_of, count, tokens.reshape(split), upstream.reshape(split), first_blocks, second_blocks)
 
 
-def grads_kernel(rows, count, xu, acts, first_grad, second_grad, turned):
+def grads_kernel(rows, count, xt, acts, first_grad, second_grad):
     panel = pl.program_id(0)
     cap = first_grad.shape[1]
-
-    @pl.when(panel == 0)
-    def _():
-        def body(r, _):
-            at = pl.ds(pl.multiple_of(r * BLOCK, BLOCK), BLOCK)
-            for a in range(2):
-                turned[a, at, :] = xu[a, :, at].T
-            return 0
-
-        lax.fori_loop(0, xu.shape[2] // BLOCK, body, 0)
 
     def one(p, _):
         at_panel = pl.ds(pl.multiple_of(p * BLOCK, BLOCK), BLOCK)
         index = panel * first_grad.shape[0] + p
         for kept in range(1, cap + 1):
 
-            @pl.when(count[index, 0] == kept)
+            @pl.when(count[index] == kept)
             def _(kept=kept):
                 for a, grad in ((0, first_grad), (1, second_grad)):
                     blocks = [
-                        turned[a, pl.ds(pl.multiple_of(rows[index, slot] * BLOCK, BLOCK), BLOCK), :]
+                        xt[a, pl.ds(pl.multiple_of(rows[slot, index] * BLOCK, BLOCK), BLOCK), :]
                         for slot in range(kept)
                     ]
                     value = jnp.dot(
@@ -576,9 +589,9 @@
     lax.fori_loop(0, first_grad.shape[0], one, 0)
 
 
-def weight_grads(xu, acts, rows, count):
-    panels, cap = rows.shape
-    tokens, width = math.prod(xu.shape[1:-1]), xu.shape[-1]
+def weight_grads(xt, acts, rows, count):
+    cap, panels = rows.shape
+    _, width, tokens = xt.shape
     block = pl.BlockSpec((GROUP, cap, BLOCK, BLOCK), lambda j, *_: (j, 0, 0, 0))
     result = jax.ShapeDtypeStruct((panels, cap, BLOCK, BLOCK), jnp.float32)
     return pl.pallas_call(
@@ -587,22 +600,20 @@
             num_scalar_prefetch=2,
             grid=(panels // GROUP,),
             in_specs=[
-                pl.BlockSpec((2, tokens, width), lambda j, *_: (0, 0, 0)),
+                pl.BlockSpec((2, width, tokens), lambda j, *_: (0, 0, 0)),
                 pl.BlockSpec((2, tokens, GROUP * BLOCK), lambda j, *_: (0, 0, j)),
             ],
             out_specs=[block, block],
-            scratch_shapes=[pltpu.VMEM((2, width, tokens), jnp.bfloat16)],
         ),
         out_shape=[result, result],
         compiler_params=pltpu.CompilerParams(vmem_limit_bytes=VMEM_LIMIT),
-    )(rows, count, xu.reshape(2, tokens, width), acts.reshape(2, tokens, panels * BLOCK))
+    )(rows, count, xt, acts.reshape(2, tokens, panels * BLOCK))
 
 
 def on_device(tokens, first_blocks, second_blocks, block_rows, block_count, upstream):
-    layer_output, grad_tokens, acts, xu = layer(
-        tokens, upstream, first_blocks, second_blocks, block_rows, block_count
-    )
-    first_grad, second_grad = weight_grads(xu, acts, block_rows, block_count)
+    rows, count = block_rows.T, block_count.reshape(-1)
+    layer_output, grad_tokens, acts, xt = layer(tokens, upstream, first_blocks, second_blocks, rows, count)
+    first_grad, second_grad = weight_grads(xt, acts, rows, count)
     return layer_output, grad_tokens, first_grad, second_grad
 
 

time: 213 us -> 211 us (level)
  local copies, waits for them, and re-layouts: 4.06 us -> 1.36 us
    pallas_call x1, Pallas kernels: 182 us -> 185 us  [layer(): pl.pallas_call(functools.partial(layer_kernel, width, hidden, cap), out_s...]
    pallas_call x1, Pallas kernels: 24.9 us -> 22.2 us  [weight_grads(): pl.pallas_call(grads_kernel, grid_spec=pltpu.PrefetchScalarGridSpec(num_s...]
    unnamed x8 -> x6, local copies, waits for them, and re-layouts: 4.06 us -> 1.36 us
where the time goes in v3:
time: 211 us; the launch traced here: 209 us
  Pallas kernels  207 us (98%)
    pallas_call x1, Pallas kernels, layer(): pl.pallas_call(functools.partial(layer_kernel, width, hidden, cap), out_s...  185 us
    pallas_call x1, Pallas kernels, weight_grads(): pl.pallas_call(grads_kernel, grid_spec=pltpu.PrefetchScalarGridSpec(num_s...  22.2 us

profile of v3, /device:TPU:2, one launch (start us, length us, event | category | flops | bytes accessed | tf_op | source)
XLA Modules:
  0.0 209.3 jit_solution(13227605779048249896)
XLA Ops:
  0.6 185.1 %shard_map.93 = (bf16[64,1536]{1,0:T(8,128)(2,1)}, bf16[64,1536]{1,0:T(8,128)(2,1)}, bf16[2,4,8,32,3072]{4,3,2,1,0:T(8,128)(2,1)}, bf16[2,1536,1024]{2,1,0:T(8,128)(2,1)}) custom-call(s32[5,24]{1,0:T(8,128)} %bitcast.8, s32[24]{0:T(128)} %bitcast.10, bf16[2,4,16,12288]{3,2,1,0:T(8,128)(2,1)} %bitcast.6, bf16[2,4,16,12288]{3,2,1,0:T(8,128)(2,1)} %bitcast.7, ...), custom_call_target="tpu_custom_call" | custom-call | tf_op jit(solution)/shard_map/pallas_call | solution.py:514
  185.7 0.0 copy-start.1
  185.7 0.0 copy-start
  185.7 22.2 %shard_map.94 = (f32[24,5,128,128]{3,2,1,0:T(8,128)}, f32[24,5,128,128]{3,2,1,0:T(8,128)}) custom-call(s32[5,24]{1,0:T(8,128)} %bitcast.9, s32[24]{0:T(128)} %bitcast.11, bf16[2,1536,1024]{2,1,0:T(8,128)(2,1)} %get-tuple-element.12.xt, bf16[2,1024,3072]{2,1,0:T(8,128)(2,1)} %bitcast.5), custom_call_target="tpu_custom_call" | custom-call | tf_op jit(solution)/shard_map/pallas_call | solution.py:597
  207.9 0.0 copy-done.1
  207.9 0.7 copy.12
  208.6 0.0 copy-done
  208.6 0.7 copy.13
Async XLA Ops:
  185.7 22.2 %copy-start.1 = (bf16[64,1536]{1,0:T(8,128)(2,1)S(1)}, bf16[64,1536]{1,0:T(8,128)(2,1)}, u32[]{:S(2)}) copy-start(bf16[64,1536]{1,0:T(8,128)(2,1)} %get-tuple-element.20) | copy-start | bytes 589828
  185.7 22.9 %copy-start = (bf16[64,1536]{1,0:T(8,128)(2,1)S(1)}, bf16[64,1536]{1,0:T(8,128)(2,1)}, u32[]{:S(2)}) copy-start(bf16[64,1536]{1,0:T(8,128)(2,1)} %get-tuple-element.21) | copy-start | bytes 589828

commit v4 on v3

--- a/solution.py
+++ b/solution.py
@@ -26,25 +26,25 @@
 )
 
 ORDER = (
-    ("dens", 0, 0), ("dens", 1, 0), ("g0", 0, 0), ("g0", 1, 0), ("g1", 0, 0), ("g1", 1, 0),
-    ("g0", 2, 0), ("g2", 0, 0), ("dens", 2, 0), ("g3", 0, 0), ("dens", 3, 0), ("dens", 4, 0),
-    ("dens", 5, 0), ("g1", 2, 0), ("g2", 1, 0), ("col", 0, 0), ("up", 0, 1), ("g3", 1, 0),
-    ("up", 0, 0), ("s1", 0, 1), ("g0", 3, 0), ("s1", 0, 0), ("g2", 2, 0), ("col", 1, 0),
-    ("up", 1, 1), ("up", 1, 0), ("s1", 1, 1), ("s2", 0, 1), ("g3", 2, 0), ("s2", 0, 0),
-    ("s1", 1, 0), ("col", 2, 0), ("g1", 3, 0), ("up", 2, 1), ("act", 0, 0), ("s2", 1, 1),
-    ("g2", 3, 0), ("s1", 2, 1), ("up", 2, 0), ("f1", 0, 1), ("s1", 2, 0), ("g3", 3, 0),
-    ("s2", 2, 1), ("f1", 0, 0), ("col", 3, 0), ("s2", 2, 0), ("up", 3, 1), ("f2", 0, 1),
-    ("s2", 1, 0), ("up", 3, 0), ("s1", 3, 1), ("act", 2, 0), ("s1", 3, 0), ("f2", 0, 0),
-    ("f1", 2, 1), ("f1", 2, 0), ("d", 0, 0), ("d", 0, 1), ("act", 1, 0), ("p3", 0, 1),
-    ("s2", 3, 0), ("s2", 3, 1), ("f2", 2, 1), ("p2", 0, 1), ("p3", 0, 0), ("f1", 1, 1),
-    ("f2", 2, 0), ("f1", 1, 0), ("d", 2, 1), ("d", 2, 0), ("p1", 0, 1), ("p2", 0, 0),
-    ("act", 3, 0), ("f2", 1, 1), ("p3", 2, 1), ("f2", 1, 0), ("p3", 2, 0), ("f1", 3, 0),
-    ("d", 1, 1), ("f1", 3, 1), ("d", 1, 0), ("f2", 3, 0), ("p1", 0, 0), ("p2", 2, 0),
-    ("p3", 1, 1), ("p3", 1, 0), ("f2", 3, 1), ("d", 3, 0), ("p2", 1, 0), ("d", 3, 1),
-    ("p2", 2, 1), ("p2", 1, 1), ("p1", 2, 1), ("p1", 2, 0), ("p1", 1, 0), ("p3", 3, 0),
-    ("p3", 3, 1), ("p0", 1, 0), ("p0", 0, 0), ("p0", 2, 1), ("p1", 1, 1), ("p2", 3, 0),
-    ("p2", 3, 1), ("p1", 3, 0), ("p1", 3, 1), ("p0", 0, 1), ("p0", 2, 0), ("p0", 1, 1),
-    ("p0", 3, 0), ("p0", 3, 1),
+    ("dens", 0, 0), ("dens", 1, 0), ("g0", 0, 0), ("g0", 2, 0), ("g1", 0, 0), ("g0", 3, 0),
+    ("g0", 1, 0), ("g1", 2, 0), ("g2", 0, 0), ("dens", 2, 0), ("g2", 2, 0), ("dens", 3, 0),
+    ("g3", 0, 0), ("g1", 1, 0), ("g1", 3, 0), ("dens", 4, 0), ("dens", 5, 0), ("g3", 2, 0),
+    ("col", 0, 0), ("up", 0, 0), ("up", 0, 1), ("col", 2, 0), ("g2", 3, 0), ("s1", 0, 0),
+    ("up", 2, 0), ("s1", 0, 1), ("g3", 3, 0), ("up", 2, 1), ("s1", 2, 0), ("s1", 2, 1),
+    ("s2", 0, 0), ("col", 3, 0), ("g2", 1, 0), ("up", 3, 0), ("s2", 0, 1), ("g3", 1, 0),
+    ("s1", 3, 0), ("s2", 2, 0), ("up", 3, 1), ("s2", 2, 1), ("act", 0, 0), ("s1", 3, 1),
+    ("col", 1, 0), ("f1", 0, 0), ("up", 1, 0), ("up", 1, 1), ("f1", 0, 1), ("s1", 1, 0),
+    ("act", 2, 0), ("s2", 3, 1), ("s1", 1, 1), ("f1", 2, 0), ("f2", 0, 0), ("s2", 3, 0),
+    ("d", 0, 0), ("s2", 1, 0), ("s2", 1, 1), ("act", 3, 0), ("p3", 0, 0), ("f2", 0, 1),
+    ("f2", 2, 0), ("f1", 2, 1), ("p2", 0, 0), ("act", 1, 0), ("f1", 3, 0), ("d", 2, 0),
+    ("d", 0, 1), ("f1", 3, 1), ("f2", 2, 1), ("p3", 2, 0), ("f1", 1, 0), ("d", 2, 1),
+    ("p2", 2, 0), ("p3", 0, 1), ("f2", 3, 0), ("f1", 1, 1), ("f2", 3, 1), ("p3", 2, 1),
+    ("d", 3, 0), ("f2", 1, 0), ("d", 3, 1), ("p2", 0, 1), ("p1", 0, 0), ("p2", 2, 1),
+    ("f2", 1, 1), ("d", 1, 0), ("p1", 2, 0), ("d", 1, 1), ("p3", 1, 0), ("p3", 3, 0),
+    ("p3", 3, 1), ("p3", 1, 1), ("p2", 1, 0), ("p2", 3, 1), ("p2", 3, 0), ("p2", 1, 1),
+    ("p0", 2, 0), ("p1", 0, 1), ("p1", 2, 1), ("p1", 3, 1), ("p0", 0, 0), ("p1", 1, 0),
+    ("p1", 3, 0), ("p1", 1, 1), ("p0", 1, 0), ("p0", 0, 1), ("p0", 2, 1), ("p0", 3, 1),
+    ("p0", 3, 0), ("p0", 1, 1),
 )
 
 

time: 211 us -> 202 us (0.957)
  Pallas kernels: 207 us -> 199 us
    pallas_call x1, Pallas kernels: 185 us -> 176 us  [layer(): pl.pallas_call(functools.partial(layer_kernel, width, hidden, cap), out_s...]
where the time goes in v4:
time: 202 us; the launch traced here: 201 us
  Pallas kernels  199 us (99%)
    pallas_call x1, Pallas kernels, layer(): pl.pallas_call(functools.partial(layer_kernel, width, hidden, cap), out_s...  176 us
    pallas_call x1, Pallas kernels, weight_grads(): pl.pallas_call(grads_kernel, grid_spec=pltpu.PrefetchScalarGridSpec(num_s...  22.5 us

profile of v4, /device:TPU:2, one launch (start us, length us, event | category | flops | bytes accessed | tf_op | source)
XLA Modules:
  0.0 201.0 jit_solution(4532408617853244717)
XLA Ops:
  0.6 176.4 %shard_map.93 = (bf16[64,1536]{1,0:T(8,128)(2,1)}, bf16[64,1536]{1,0:T(8,128)(2,1)}, bf16[2,4,8,32,3072]{4,3,2,1,0:T(8,128)(2,1)}, bf16[2,1536,1024]{2,1,0:T(8,128)(2,1)}) custom-call(s32[5,24]{1,0:T(8,128)} %bitcast.8, s32[24]{0:T(128)} %bitcast.10, bf16[2,4,16,12288]{3,2,1,0:T(8,128)(2,1)} %bitcast.6, bf16[2,4,16,12288]{3,2,1,0:T(8,128)(2,1)} %bitcast.7, ...), custom_call_target="tpu_custom_call" | custom-call | tf_op jit(solution)/shard_map/pallas_call | solution.py:514
  177.1 0.0 copy-start.1
  177.1 0.0 copy-start
  177.1 22.5 %shard_map.94 = (f32[24,5,128,128]{3,2,1,0:T(8,128)}, f32[24,5,128,128]{3,2,1,0:T(8,128)}) custom-call(s32[5,24]{1,0:T(8,128)} %bitcast.9, s32[24]{0:T(128)} %bitcast.11, bf16[2,1536,1024]{2,1,0:T(8,128)(2,1)} %get-tuple-element.12.xt, bf16[2,1024,3072]{2,1,0:T(8,128)(2,1)} %bitcast.5), custom_call_target="tpu_custom_call" | custom-call | tf_op jit(solution)/shard_map/pallas_call | solution.py:597
  199.6 0.0 copy-done.1
  199.6 0.7 copy.12
  200.3 0.0 copy-done
  200.3 0.7 copy.13
Async XLA Ops:
  177.1 22.5 %copy-start.1 = (bf16[64,1536]{1,0:T(8,128)(2,1)S(1)}, bf16[64,1536]{1,0:T(8,128)(2,1)}, u32[]{:S(2)}) copy-start(bf16[64,1536]{1,0:T(8,128)(2,1)} %get-tuple-element.20) | copy-start | bytes 589828
  177.1 23.2 %copy-start = (bf16[64,1536]{1,0:T(8,128)(2,1)S(1)}, bf16[64,1536]{1,0:T(8,128)(2,1)}, u32[]{:S(2)}) copy-start(bf16[64,1536]{1,0:T(8,128)(2,1)} %get-tuple-element.21) | copy-start | bytes 589828
